TPU v7x, 256 devices: a whole 4x4x8 slice. The times are simulated.
256 devices in a mesh: seg: 16 (over x_lo, z), head: 8 (over y, core), section: 2 (over x_hi).
Axes of the slice: x: 4 (x_hi: 2, x_lo: 2; x = x_hi * 2 + x_lo), y: 4, z: 8, core: 2. Of those that a mesh axis runs over, the one named last changes fastest.
Arguments:
- tokens: bfloat16 [3072, 3072], P('seg', 'head'), may hold values from -6 to 6
- in_weight: bfloat16 [2, 3, 3072, 3072], P('section', None, None, 'head'), may hold values from -0.109375 to 0.109375
- out_weight: bfloat16 [2, 3072, 3072], P('section', 'head'), may hold values from -0.109375 to 0.109375
- expand_init: float32 [2, 2, 48, 64, 128], P('section', None, 'head'), may hold values from -0.75 to 0.75
- contract_init: float32 [2, 2, 48, 128, 64], P('section', None, 'head'), may hold values from -0.5 to 0.5
- inner_rate: float32 [2, 2, 48], P('section', None, 'head'), may hold values from 0.1 to 1
- seg_counts: int32 [16], P('seg'), may hold values from 1 to 192, 2304 in all
Outputs:
- panels: bfloat16 [2, 3072, 3072], P('section', 'seg', 'head')
Inputs may be any that keep to these rules, and one draw needn't show every extreme that they name: The live tokens of segment s are its first seg_counts[s]; the counts sum to 2304 and the largest equals 192.
All inputs are finite; a program needn't handle non-finite values. No bound on the sum of `seg_counts` on one device may be relied on, other than what follows from the above.
Results may differ from a plain program's by a relative error of at most 0.027.
Values may be sent and summed in bfloat16 or wider, within the bound.
A program may use at most 128 MiB of HBM per device.

v0:
```python
import math

import jax
import jax.numpy as jnp
from jax import lax
from jax.sharding import PartitionSpec as P

MB = 64


highest = lax.Precision.HIGHEST
gelu_coef = math.sqrt(2.0 / math.pi)
cubic_coef = 0.044715


def from_behind(block, axis, distance):
    devices = range(lax.axis_size(axis))
    route = [(i - distance, i) for i in devices if i - distance in devices]
    return lax.ppermute(block, axis, route)


def smooth(preact):
    return (
        0.5
        * preact
        * (1.0 + jnp.tanh(gelu_coef * (preact + cubic_coef * preact * preact * preact)))
    )


def slope(preact):
    curved = jnp.tanh(gelu_coef * (preact + cubic_coef * preact * preact * preact))
    return 0.5 * (1.0 + curved) + 0.5 * preact * (1.0 - curved * curved) * gelu_coef * (
        1.0 + 3.0 * cubic_coef * preact * preact
    )


def rescale(rows):
    return rows * lax.rsqrt(jnp.mean(rows * rows, axis=-1, keepdims=True) + 1e-06)


def inner_step(state, key_rows, value_rows, query_rows, live_rows, rate):
    batch_rows = key_rows.shape[0]
    step_rate = rate / key_rows.shape[2]
    preact = jnp.einsum("mhe,hef->mhf", key_rows, state[0], precision=highest)
    active = smooth(preact)
    predicted = key_rows + jnp.einsum("mhf,hef->mhe", active, state[1], precision=highest)
    misfit = (predicted - value_rows) * (live_rows / batch_rows)[:, None, None]
    backflow = jnp.einsum("mhe,hef->mhf", misfit, state[1], precision=highest) * slope(preact)
    grad_expand = jnp.einsum("mhe,mhf->hef", key_rows, backflow, precision=highest)
    grad_contract = jnp.einsum("mhe,mhf->hef", misfit, active, precision=highest)
    updated = state - step_rate[None, :, None, None] * jnp.stack([grad_expand, grad_contract])
    lifted = smooth(jnp.einsum("mhe,hef->mhf", query_rows, updated[0], precision=highest))
    result = query_rows + jnp.einsum("mhf,hef->mhe", lifted, updated[1], precision=highest)
    return (updated, result)


def run_blocks(state, key_all, value_all, query_all, live_all, rate, backward):

    def step(carry, pieces):
        return inner_step(carry, pieces[0], pieces[1], pieces[2], pieces[3], rate)

    final, results = lax.scan(
        step, state, (key_all, value_all, query_all, live_all), reverse=backward
    )
    return (final, results)


def fast_weights(projected, expand, contract, rates, live_mask):
    rounded = lax.optimization_barrier(projected.astype(jnp.bfloat16))
    head_count = expand.shape[1]
    head_width = expand.shape[2]
    fast_units = expand.shape[3]
    row_count = projected.shape[1]
    blocks = row_count // MB
    shaped = rounded.astype(jnp.float32).reshape(3, blocks, MB, head_count, head_width)
    query_all = rescale(shaped[0])
    key_all = rescale(shaped[1])
    value_all = rescale(shaped[2])
    live_all = live_mask.reshape(blocks, MB)
    starts = jnp.stack(
        [
            jnp.stack([expand[0], jnp.swapaxes(contract[0], 1, 2)]),
            jnp.stack([expand[1], jnp.swapaxes(contract[1], 1, 2)]),
        ]
    )
    seg_index = lax.axis_index("seg")
    seg_count = lax.axis_size("seg")
    groups = head_count // head_count
    turns = seg_count + groups - 1

    def advance(turn_at, carried, direction):
        received, outputs = carried
        if direction == 0:
            lag = seg_index
        else:
            lag = seg_count - 1 - seg_index
        group = turn_at - lag
        valid = (group >= 0) & (group < groups)
        begin = starts[direction]
        state = jnp.where(lag == 0, begin, received)

        def work(operand):
            state_now, outputs_now = operand
            rate = rates[direction]
            final, result = run_blocks(
                state_now, key_all, value_all, query_all, live_all, rate, direction == 1
            )
            return (final, result)

        def keep(operand):
            return operand

        return lax.cond(valid, work, keep, (state, outputs))

    def both(turn_at, carried):
        return (advance(turn_at, carried[0], 0), advance(turn_at, carried[1], 1))

    def hop(turn_at, carried):
        forward, backward = both(turn_at, carried)
        sent_forward = from_behind(forward[0].astype(jnp.bfloat16), "seg", 1).astype(jnp.float32)
        sent_backward = from_behind(backward[0].astype(jnp.bfloat16), "seg", -1).astype(jnp.float32)
        return ((sent_forward, forward[1]), (sent_backward, backward[1]))

    empty_state = jnp.zeros((2, head_count, head_width, fast_units), jnp.float32)
    empty_out = jnp.zeros((blocks, MB, head_count, head_width), jnp.float32)
    carried = ((empty_state, empty_out), (empty_state, empty_out))
    carried = lax.fori_loop(0, turns - 1, hop, carried)
    forward, backward = both(turns - 1, carried)
    return (
        (forward[1] + backward[1]).reshape(row_count, head_count * head_width).astype(jnp.bfloat16)
    )


def layer(hidden, weights):
    in_w, out_rows, expand, contract, rates, live_mask = weights
    projected = jnp.einsum(
        "td,jdc->jtc",
        lax.all_gather(hidden, "head", axis=1, tiled=True),
        in_w,
        preferred_element_type=jnp.float32,
    )
    mixture = fast_weights(projected, expand, contract, rates, live_mask)
    term = jnp.dot(mixture, out_rows, preferred_element_type=jnp.float32)
    summed = lax.psum_scatter(
        term.astype(jnp.bfloat16), "head", scatter_dimension=1, tiled=True
    ).astype(jnp.float32)
    return (hidden.astype(jnp.float32) + summed).astype(jnp.bfloat16)


def local(tokens, in_weight, out_weight, expand_init, contract_init, inner_rate, seg_counts):
    row_count = tokens.shape[0]
    position = lax.broadcasted_iota(jnp.int32, (row_count,), 0)
    live_mask = (position < seg_counts[0]).astype(jnp.float32)
    out_rows = out_weight[0]
    weights = (in_weight[0], out_rows, expand_init[0], contract_init[0], inner_rate[0], live_mask)
    earlier = layer(tokens, weights)
    handed = from_behind(earlier, "section", 1)
    later = layer(handed, weights)
    panel = jnp.where(lax.axis_index("section") == 0, earlier, later)
    return panel[None]


def solution(mesh):
    placed = (
        P("seg", "head"),
        P("section", None, None, "head"),
        P("section", "head", None),
        P("section", None, "head", None, None),
        P("section", None, "head", None, None),
        P("section", None, "head"),
        P("seg"),
    )
    return jax.shard_map(
        local, mesh=mesh, in_specs=placed, out_specs=P("section", "seg", "head"), check_vma=False
    )
```

profile of v0, /device:TPU:4, one launch (start us, length us, event | category | flops | bytes accessed | tf_op | source)
XLA Modules:
  0.0 1303.3 jit_solution(18132634313922113454)
XLA Ops:
  11.0 27.3 %all-gather.3.cloned.1.call-done = bf16[192,3072]{1,0:T(8,128)(2,1)} async-done(((bf16[192,384]{1,0:T(8,128)(2,1)}), bf16[192,3072]{1,0:T(8,128)(2,1)}) %all-gather.3.cloned.1.call-update) | async-done | bytes 1179664 | tf_op jit(solution)/shard_map/all_gather | solution.py:138
  38.4 5.1 fusion.437
  70.3 484.9 %while.166 = (s32[]{:T(128)}, f32[2,6,64,128]{3,2,1,0:T(8,128)S(1)}, f32[3,64,6,64]{3,1,2,0:T(8,128)}, f32[2,6,64,128]{3,2,1,0:T(8,128)}, f32[3,64,6,64]{3,1,2,0...) while((s32[]{:T(128)}, f32[2,6,64,128]{3,2,1,0:T(8,128)S(1)}, ...), condition=%wide.region_12.13_spmd.clone, body=%wide.region_3.12_spmd.clone.sunk | while | flops 534184832 | bytes 20354724 | solution.py:127
  73.5 20.4 %conditional.20 = ((f32[2,6,64,128]{3,2,1,0:T(8,128)S(1)}, f32[3,64,6,64]{3,1,2,0:T(8,128)})) conditional(s32[]{:T(128)} %convert_element_type.249, (f32[2,6,64,128]{3,2,1,0:T(8,128)S(1)}, f32[3,64,6,64]{3,1,2,0:T(8,128)}) %tuple.327, (f32[2,6]{1,0:T(2,128)S(1)}, f32[3,64,6,64]{3,1,2,0:T(8,128)}, f32[3,64,6,64]{3,1,2,0:T(8,128)}, ...), branch_computations={%region_4.4_spmd, %region_5.7_spmd} | conditional | flops 266698816 | bytes 6884197 | solution.py:113
  73.5 20.4 %while.158 = (s32[]{:T(128)}, f32[2,6,64,128]{3,2,1,0:T(8,128)S(1)}, f32[3,64,6,64]{3,1,2,0:T(8,128)}, f32[6]{0:T(128)S(1)}, f32[3,64,6,64]{3,1,2,0:T(8,128)}, /...) while((s32[]{:T(128)}, f32[2,6,64,128]{3,2,1,0:T(8,128)S(1)}, ...), condition=%wide.region_7.6_spmd, body=%wide.region_6.5_spmd.sunk | while | flops 266698816 | bytes 6884045 | solution.py:62
  103.5 25.3 %collective-permute-start.2 = (bf16[2,6,64,128]{3,2,1,0:T(8,128)(2,1)S(1)}, bf16[2,6,64,128]{3,2,1,0:T(8,128)(2,1)S(1)}, u32[]{:S(2)}, u32[]{:S(2)}) collective-permute-start(bf16[2,6,64,128]{3,2,1,0:T(8,128)(2,1)S(1)} %convert_element_type.250), channel_id=1, source_target_pairs={{0,16},{16,32},{32,48},{48,64},{64,80},{80,96},{96,112},{112,128},... | collective-permute-start | bytes 589832 | tf_op jit(solution)/shard_map/while/body/eval_jaxpr/ppermute | solution.py:19
  136.3 4.9 collective-permute-start.2
  148.4 24.3 %collective-permute-start.2 = (bf16[2,6,64,128]{3,2,1,0:T(8,128)(2,1)S(1)}, bf16[2,6,64,128]{3,2,1,0:T(8,128)(2,1)S(1)}, u32[]{:S(2)}, u32[]{:S(2)}) collective-permute-start(bf16[2,6,64,128]{3,2,1,0:T(8,128)(2,1)S(1)} %convert_element_type.250), channel_id=1, source_target_pairs={{0,16},{16,32},{32,48},{48,64},{64,80},{80,96},{96,112},{112,128},... | collective-permute-start | bytes 589832 | tf_op jit(solution)/shard_map/while/body/eval_jaxpr/ppermute | solution.py:19
  179.5 4.9 collective-permute-start.2
  191.3 24.6 %collective-permute-start.2 = (bf16[2,6,64,128]{3,2,1,0:T(8,128)(2,1)S(1)}, bf16[2,6,64,128]{3,2,1,0:T(8,128)(2,1)S(1)}, u32[]{:S(2)}, u32[]{:S(2)}) collective-permute-start(bf16[2,6,64,128]{3,2,1,0:T(8,128)(2,1)S(1)} %convert_element_type.250), channel_id=1, source_target_pairs={{0,16},{16,32},{32,48},{48,64},{64,80},{80,96},{96,112},{112,128},... | collective-permute-start | bytes 589832 | tf_op jit(solution)/shard_map/while/body/eval_jaxpr/ppermute | solution.py:19
  222.7 4.9 collective-permute-start.2
  234.5 25.8 %collective-permute-start.2 = (bf16[2,6,64,128]{3,2,1,0:T(8,128)(2,1)S(1)}, bf16[2,6,64,128]{3,2,1,0:T(8,128)(2,1)S(1)}, u32[]{:S(2)}, u32[]{:S(2)}) collective-permute-start(bf16[2,6,64,128]{3,2,1,0:T(8,128)(2,1)S(1)} %convert_element_type.250), channel_id=1, source_target_pairs={{0,16},{16,32},{32,48},{48,64},{64,80},{80,96},{96,112},{112,128},... | collective-permute-start | bytes 589832 | tf_op jit(solution)/shard_map/while/body/eval_jaxpr/ppermute | solution.py:19
  267.2 6.1 collective-permute-start.2
  280.2 24.6 %collective-permute-start.2 = (bf16[2,6,64,128]{3,2,1,0:T(8,128)(2,1)S(1)}, bf16[2,6,64,128]{3,2,1,0:T(8,128)(2,1)S(1)}, u32[]{:S(2)}, u32[]{:S(2)}) collective-permute-start(bf16[2,6,64,128]{3,2,1,0:T(8,128)(2,1)S(1)} %convert_element_type.250), channel_id=1, source_target_pairs={{0,16},{16,32},{32,48},{48,64},{64,80},{80,96},{96,112},{112,128},... | collective-permute-start | bytes 589832 | tf_op jit(solution)/shard_map/while/body/eval_jaxpr/ppermute | solution.py:19
  311.9 5.5 collective-permute-start.2
  324.3 26.6 %collective-permute-start.2 = (bf16[2,6,64,128]{3,2,1,0:T(8,128)(2,1)S(1)}, bf16[2,6,64,128]{3,2,1,0:T(8,128)(2,1)S(1)}, u32[]{:S(2)}, u32[]{:S(2)}) collective-permute-start(bf16[2,6,64,128]{3,2,1,0:T(8,128)(2,1)S(1)} %convert_element_type.250), channel_id=1, source_target_pairs={{0,16},{16,32},{32,48},{48,64},{64,80},{80,96},{96,112},{112,128},... | collective-permute-start | bytes 589832 | tf_op jit(solution)/shard_map/while/body/eval_jaxpr/ppermute | solution.py:19
  350.9 3.3 collective-permute-done.3
  359.3 4.6 collective-permute-start.2
  370.7 20.4 %collective-permute-start.2 = (bf16[2,6,64,128]{3,2,1,0:T(8,128)(2,1)S(1)}, bf16[2,6,64,128]{3,2,1,0:T(8,128)(2,1)S(1)}, u32[]{:S(2)}, u32[]{:S(2)}) collective-permute-start(bf16[2,6,64,128]{3,2,1,0:T(8,128)(2,1)S(1)} %convert_element_type.250), channel_id=1, source_target_pairs={{0,16},{16,32},{32,48},{48,64},{64,80},{80,96},{96,112},{112,128},... | collective-permute-start | bytes 589832 | tf_op jit(solution)/shard_map/while/body/eval_jaxpr/ppermute | solution.py:19
  398.0 153.6 %collective-permute-start.2 = (bf16[2,6,64,128]{3,2,1,0:T(8,128)(2,1)S(1)}, bf16[2,6,64,128]{3,2,1,0:T(8,128)(2,1)S(1)}, u32[]{:S(2)}, u32[]{:S(2)}) collective-permute-start(bf16[2,6,64,128]{3,2,1,0:T(8,128)(2,1)S(1)} %convert_element_type.250), channel_id=1, source_target_pairs={{0,16},{16,32},{32,48},{48,64},{64,80},{80,96},{96,112},{112,128},... | collective-permute-start | bytes 589832 | tf_op jit(solution)/shard_map/while/body/eval_jaxpr/ppermute | solution.py:19
  555.9 20.3 %conditional.9 = (f32[3,64,6,64]{3,1,2,0:T(8,128)}) conditional(s32[]{:T(128)} %convert_element_type.168, f32[3,64,6,64]{3,1,2,0:T(8,128)} %get-tuple-element.1607, (pred[]{:T(512)}, f32[2,6,64,128]{3,2,1,0:T(8,128)}, f32[2,6,64,128]{3,2,1,0:T(8,128)}, f32[2,6]{1,0:T(2,128)}, f32[3,64,6,64]{3,2,1,0:T(8,128)}, ...), branch_computations={%region_17.18_spmd, %region_18.21_spmd} | conditional | flops 266797120 | bytes 12977814 | solution.py:113
  561.7 14.5 %while.161 = (s32[]{:T(128)}, f32[2,6,64,128]{3,2,1,0:T(8,128)S(1)}, f32[3,64,6,64]{3,1,2,0:T(8,128)}, f32[6]{0:T(128)S(1)}, f32[3,64,6,64]{3,1,2,0:T(8,128)S(1)...) while((s32[]{:T(128)}, f32[2,6,64,128]{3,2,1,0:T(8,128)S(1)}, ...), condition=%wide.region_20.20_spmd, body=%wide.region_19.19_spmd.sunk | while | flops 266698816 | bytes 6980845 | solution.py:62
  582.0 65.5 %reduce-scatter.7.cloned.1.call-done = bf16[384,192]{1,0:T(8,128)(2,1)} async-done(((bf16[3072,192]{1,0:T(8,128)(2,1)}), bf16[384,192]{1,0:T(8,128)(2,1)}) %reduce-scatter.7.cloned.1.call-update) | async-done | bytes 147472
  651.4 7.2 collective-permute-done.4
  659.6 25.2 %all-gather.5.cloned.1.call-done = bf16[192,3072]{1,0:T(8,128)(2,1)} async-done(((bf16[192,384]{1,0:T(8,128)(2,1)}), bf16[192,3072]{1,0:T(8,128)(2,1)}) %all-gather.5.cloned.1.call-update) | async-done | bytes 1179664 | tf_op jit(solution)/shard_map/all_gather | solution.py:138
  684.8 5.1 fusion.434
  716.9 482.8 %while.167 = (s32[]{:T(128)}, f32[2,6,64,128]{3,2,1,0:T(8,128)S(1)}, f32[3,64,6,64]{3,1,2,0:T(8,128)}, f32[2,6,64,128]{3,2,1,0:T(8,128)}, f32[3,64,6,64]{3,1,2,0...) while((s32[]{:T(128)}, f32[2,6,64,128]{3,2,1,0:T(8,128)S(1)}, ...), condition=%wide.region_34.35_spmd.clone, body=%wide.region_25.34_spmd.clone.sunk | while | flops 534184832 | bytes 20354724 | solution.py:127
  720.1 20.4 %conditional.22 = ((f32[2,6,64,128]{3,2,1,0:T(8,128)S(1)}, f32[3,64,6,64]{3,1,2,0:T(8,128)})) conditional(s32[]{:T(128)} %convert_element_type.256, (f32[2,6,64,128]{3,2,1,0:T(8,128)S(1)}, f32[3,64,6,64]{3,1,2,0:T(8,128)}) %tuple.333, (f32[2,6]{1,0:T(2,128)S(1)}, f32[3,64,6,64]{3,1,2,0:T(8,128)}, f32[3,64,6,64]{3,1,2,0:T(8,128)}, ...), branch_computations={%region_26.26_spmd, %region_27.29_spmd} | conditional | flops 266698816 | bytes 6884197 | solution.py:113
  720.1 20.4 %while.162 = (s32[]{:T(128)}, f32[2,6,64,128]{3,2,1,0:T(8,128)S(1)}, f32[3,64,6,64]{3,1,2,0:T(8,128)}, f32[6]{0:T(128)S(1)}, f32[3,64,6,64]{3,1,2,0:T(8,128)}, /...) while((s32[]{:T(128)}, f32[2,6,64,128]{3,2,1,0:T(8,128)S(1)}, ...), condition=%wide.region_29.28_spmd, body=%wide.region_28.27_spmd.sunk | while | flops 266698816 | bytes 6884045 | solution.py:62
  742.7 4.0 collective-permute-done
  750.1 25.3 %collective-permute-start = (bf16[2,6,64,128]{3,2,1,0:T(8,128)(2,1)S(1)}, bf16[2,6,64,128]{3,2,1,0:T(8,128)(2,1)S(1)}, u32[]{:S(2)}, u32[]{:S(2)}) collective-permute-start(bf16[2,6,64,128]{3,2,1,0:T(8,128)(2,1)S(1)} %convert_element_type.257), channel_id=1, source_target_pairs={{0,16},{16,32},{32,48},{48,64},{64,80},{80,96},{96,112},{112,128},... | collective-permute-start | bytes 589832 | tf_op jit(solution)/shard_map/while/body/eval_jaxpr/ppermute | solution.py:19
  776.3 3.3 collective-permute-done
  782.9 4.9 collective-permute-start
  794.4 24.8 %collective-permute-start = (bf16[2,6,64,128]{3,2,1,0:T(8,128)(2,1)S(1)}, bf16[2,6,64,128]{3,2,1,0:T(8,128)(2,1)S(1)}, u32[]{:S(2)}, u32[]{:S(2)}) collective-permute-start(bf16[2,6,64,128]{3,2,1,0:T(8,128)(2,1)S(1)} %convert_element_type.257), channel_id=1, source_target_pairs={{0,16},{16,32},{32,48},{48,64},{64,80},{80,96},{96,112},{112,128},... | collective-permute-start | bytes 589832 | tf_op jit(solution)/shard_map/while/body/eval_jaxpr/ppermute | solution.py:19
  825.8 4.9 collective-permute-start
  837.3 24.9 %collective-permute-start = (bf16[2,6,64,128]{3,2,1,0:T(8,128)(2,1)S(1)}, bf16[2,6,64,128]{3,2,1,0:T(8,128)(2,1)S(1)}, u32[]{:S(2)}, u32[]{:S(2)}) collective-permute-start(bf16[2,6,64,128]{3,2,1,0:T(8,128)(2,1)S(1)} %convert_element_type.257), channel_id=1, source_target_pairs={{0,16},{16,32},{32,48},{48,64},{64,80},{80,96},{96,112},{112,128},... | collective-permute-start | bytes 589832 | tf_op jit(solution)/shard_map/while/body/eval_jaxpr/ppermute | solution.py:19
  868.8 4.9 collective-permute-start
  880.3 26.1 %collective-permute-start = (bf16[2,6,64,128]{3,2,1,0:T(8,128)(2,1)S(1)}, bf16[2,6,64,128]{3,2,1,0:T(8,128)(2,1)S(1)}, u32[]{:S(2)}, u32[]{:S(2)}) collective-permute-start(bf16[2,6,64,128]{3,2,1,0:T(8,128)(2,1)S(1)} %convert_element_type.257), channel_id=1, source_target_pairs={{0,16},{16,32},{32,48},{48,64},{64,80},{80,96},{96,112},{112,128},... | collective-permute-start | bytes 589832 | tf_op jit(solution)/shard_map/while/body/eval_jaxpr/ppermute | solution.py:19
  912.9 6.1 collective-permute-start
  925.6 24.9 %collective-permute-start = (bf16[2,6,64,128]{3,2,1,0:T(8,128)(2,1)S(1)}, bf16[2,6,64,128]{3,2,1,0:T(8,128)(2,1)S(1)}, u32[]{:S(2)}, u32[]{:S(2)}) collective-permute-start(bf16[2,6,64,128]{3,2,1,0:T(8,128)(2,1)S(1)} %convert_element_type.257), channel_id=1, source_target_pairs={{0,16},{16,32},{32,48},{48,64},{64,80},{80,96},{96,112},{112,128},... | collective-permute-start | bytes 589832 | tf_op jit(solution)/shard_map/while/body/eval_jaxpr/ppermute | solution.py:19
  957.6 5.6 collective-permute-start
  969.7 28.6 %collective-permute-start = (bf16[2,6,64,128]{3,2,1,0:T(8,128)(2,1)S(1)}, bf16[2,6,64,128]{3,2,1,0:T(8,128)(2,1)S(1)}, u32[]{:S(2)}, u32[]{:S(2)}) collective-permute-start(bf16[2,6,64,128]{3,2,1,0:T(8,128)(2,1)S(1)} %convert_element_type.257), channel_id=1, source_target_pairs={{0,16},{16,32},{32,48},{48,64},{64,80},{80,96},{96,112},{112,128},... | collective-permute-start | bytes 589832 | tf_op jit(solution)/shard_map/while/body/eval_jaxpr/ppermute | solution.py:19
  1005.6 4.9 collective-permute-start
  1017.1 19.1 %collective-permute-start = (bf16[2,6,64,128]{3,2,1,0:T(8,128)(2,1)S(1)}, bf16[2,6,64,128]{3,2,1,0:T(8,128)(2,1)S(1)}, u32[]{:S(2)}, u32[]{:S(2)}) collective-permute-start(bf16[2,6,64,128]{3,2,1,0:T(8,128)(2,1)S(1)} %convert_element_type.257), channel_id=1, source_target_pairs={{0,16},{16,32},{32,48},{48,64},{64,80},{80,96},{96,112},{112,128},... | collective-permute-start | bytes 589832 | tf_op jit(solution)/shard_map/while/body/eval_jaxpr/ppermute | solution.py:19
  1042.9 153.6 %collective-permute-start = (bf16[2,6,64,128]{3,2,1,0:T(8,128)(2,1)S(1)}, bf16[2,6,64,128]{3,2,1,0:T(8,128)(2,1)S(1)}, u32[]{:S(2)}, u32[]{:S(2)}) collective-permute-start(bf16[2,6,64,128]{3,2,1,0:T(8,128)(2,1)S(1)} %convert_element_type.257), channel_id=1, source_target_pairs={{0,16},{16,32},{32,48},{48,64},{64,80},{80,96},{96,112},{112,128},... | collective-permute-start | bytes 589832 | tf_op jit(solution)/shard_map/while/body/eval_jaxpr/ppermute | solution.py:19
  1200.4 20.0 %conditional.11 = (f32[3,64,6,64]{3,1,2,0:T(8,128)}) conditional(s32[]{:T(128)} %convert_element_type.168, f32[3,64,6,64]{3,1,2,0:T(8,128)} %get-tuple-element.1611, (pred[]{:T(512)}, f32[2,6,64,128]{3,2,1,0:T(8,128)}, f32[2,6,64,128]{3,2,1,0:T(8,128)}, f32[2,6]{1,0:T(2,128)}, f32[3,64,6,64]{3,2,1,0:T(8,128)}, ...), branch_computations={%region_39.40_spmd, %region_40.43_spmd} | conditional | flops 266797120 | bytes 12977814 | solution.py:113
  1205.9 14.5 %while.165 = (s32[]{:T(128)}, f32[2,6,64,128]{3,2,1,0:T(8,128)S(1)}, f32[3,64,6,64]{3,1,2,0:T(8,128)}, f32[6]{0:T(128)S(1)}, f32[3,64,6,64]{3,1,2,0:T(8,128)S(1)...) while((s32[]{:T(128)}, f32[2,6,64,128]{3,2,1,0:T(8,128)S(1)}, ...), condition=%wide.region_42.42_spmd, body=%wide.region_41.41_spmd.sunk | while | flops 266698816 | bytes 6980845 | solution.py:62
  1226.2 67.6 %reduce-scatter.9.cloned.1.call-done = bf16[384,192]{1,0:T(8,128)(2,1)} async-done(((bf16[3072,192]{1,0:T(8,128)(2,1)}), bf16[384,192]{1,0:T(8,128)(2,1)}) %reduce-scatter.9.cloned.1.call-update) | async-done | bytes 147472
  (661 shorter events, 355.5 us)
Async XLA Ops:
  6.5 31.9 %all-gather.3.cloned.1.call-start = ((), (), s32[]{:S(2)}) async-start(), calls=%async_computation.2 | async-start | bytes 1327104 | tf_op jit(solution)/shard_map/all_gather | solution.py:138
  7.3 640.2 %reduce-scatter.7.cloned.1.call-start = ((), (), s32[]{:S(2)}) async-start(), calls=%async_computation.4 | async-start | bytes 1769472
  72.1 23.1 %collective-permute-start.3 = (bf16[2,6,64,128]{3,2,1,0:T(8,128)(2,1)S(1)}, bf16[2,6,64,128]{3,2,1,0:T(8,128)(2,1)}, u32[]{:S(2)}, u32[]{:S(2)}) collective-permute-start(bf16[2,6,64,128]{3,2,1,0:T(8,128)(2,1)S(1)} %convert_element_type.253), channel_id=1, source_target_pairs={{16,0},{32,16},{48,32},{64,48},{80,64},{96,80},{112,96},{128,112},... | collective-permute-start | bytes 589832 | tf_op jit(solution)/shard_map/while/body/eval_jaxpr/ppermute | solution.py:19
  102.1 26.7 %collective-permute-start.3 = (bf16[2,6,64,128]{3,2,1,0:T(8,128)(2,1)S(1)}, bf16[2,6,64,128]{3,2,1,0:T(8,128)(2,1)}, u32[]{:S(2)}, u32[]{:S(2)}) collective-permute-start(bf16[2,6,64,128]{3,2,1,0:T(8,128)(2,1)S(1)} %convert_element_type.253), channel_id=1, source_target_pairs={{16,0},{32,16},{48,32},{64,48},{80,64},{96,80},{112,96},{128,112},... | collective-permute-start | bytes 589832 | tf_op jit(solution)/shard_map/while/body/eval_jaxpr/ppermute | solution.py:19
  103.5 29.4 %collective-permute-start.2 = (bf16[2,6,64,128]{3,2,1,0:T(8,128)(2,1)S(1)}, bf16[2,6,64,128]{3,2,1,0:T(8,128)(2,1)S(1)}, u32[]{:S(2)}, u32[]{:S(2)}) collective-permute-start(bf16[2,6,64,128]{3,2,1,0:T(8,128)(2,1)S(1)} %convert_element_type.250), channel_id=1, source_target_pairs={{0,16},{16,32},{32,48},{48,64},{64,80},{80,96},{96,112},{112,128},... | collective-permute-start | bytes 589832 | tf_op jit(solution)/shard_map/while/body/eval_jaxpr/ppermute | solution.py:19
  136.3 8.7 collective-permute-start.2
  147.0 27.4 %collective-permute-start.3 = (bf16[2,6,64,128]{3,2,1,0:T(8,128)(2,1)S(1)}, bf16[2,6,64,128]{3,2,1,0:T(8,128)(2,1)}, u32[]{:S(2)}, u32[]{:S(2)}) collective-permute-start(bf16[2,6,64,128]{3,2,1,0:T(8,128)(2,1)S(1)} %convert_element_type.253), channel_id=1, source_target_pairs={{16,0},{32,16},{48,32},{64,48},{80,64},{96,80},{112,96},{128,112},... | collective-permute-start | bytes 589832 | tf_op jit(solution)/shard_map/while/body/eval_jaxpr/ppermute | solution.py:19
  148.4 27.7 %collective-permute-start.2 = (bf16[2,6,64,128]{3,2,1,0:T(8,128)(2,1)S(1)}, bf16[2,6,64,128]{3,2,1,0:T(8,128)(2,1)S(1)}, u32[]{:S(2)}, u32[]{:S(2)}) collective-permute-start(bf16[2,6,64,128]{3,2,1,0:T(8,128)(2,1)S(1)} %convert_element_type.250), channel_id=1, source_target_pairs={{0,16},{16,32},{32,48},{48,64},{64,80},{80,96},{96,112},{112,128},... | collective-permute-start | bytes 589832 | tf_op jit(solution)/shard_map/while/body/eval_jaxpr/ppermute | solution.py:19
  189.9 27.7 %collective-permute-start.3 = (bf16[2,6,64,128]{3,2,1,0:T(8,128)(2,1)S(1)}, bf16[2,6,64,128]{3,2,1,0:T(8,128)(2,1)}, u32[]{:S(2)}, u32[]{:S(2)}) collective-permute-start(bf16[2,6,64,128]{3,2,1,0:T(8,128)(2,1)S(1)} %convert_element_type.253), channel_id=1, source_target_pairs={{16,0},{32,16},{48,32},{64,48},{80,64},{96,80},{112,96},{128,112},... | collective-permute-start | bytes 589832 | tf_op jit(solution)/shard_map/while/body/eval_jaxpr/ppermute | solution.py:19
  191.3 28.0 %collective-permute-start.2 = (bf16[2,6,64,128]{3,2,1,0:T(8,128)(2,1)S(1)}, bf16[2,6,64,128]{3,2,1,0:T(8,128)(2,1)S(1)}, u32[]{:S(2)}, u32[]{:S(2)}) collective-permute-start(bf16[2,6,64,128]{3,2,1,0:T(8,128)(2,1)S(1)} %convert_element_type.250), channel_id=1, source_target_pairs={{0,16},{16,32},{32,48},{48,64},{64,80},{80,96},{96,112},{112,128},... | collective-permute-start | bytes 589832 | tf_op jit(solution)/shard_map/while/body/eval_jaxpr/ppermute | solution.py:19
  233.2 28.9 %collective-permute-start.3 = (bf16[2,6,64,128]{3,2,1,0:T(8,128)(2,1)S(1)}, bf16[2,6,64,128]{3,2,1,0:T(8,128)(2,1)}, u32[]{:S(2)}, u32[]{:S(2)}) collective-permute-start(bf16[2,6,64,128]{3,2,1,0:T(8,128)(2,1)S(1)} %convert_element_type.253), channel_id=1, source_target_pairs={{16,0},{32,16},{48,32},{64,48},{80,64},{96,80},{112,96},{128,112},... | collective-permute-start | bytes 589832 | tf_op jit(solution)/shard_map/while/body/eval_jaxpr/ppermute | solution.py:19
  234.5 29.2 %collective-permute-start.2 = (bf16[2,6,64,128]{3,2,1,0:T(8,128)(2,1)S(1)}, bf16[2,6,64,128]{3,2,1,0:T(8,128)(2,1)S(1)}, u32[]{:S(2)}, u32[]{:S(2)}) collective-permute-start(bf16[2,6,64,128]{3,2,1,0:T(8,128)(2,1)S(1)} %convert_element_type.250), channel_id=1, source_target_pairs={{0,16},{16,32},{32,48},{48,64},{64,80},{80,96},{96,112},{112,128},... | collective-permute-start | bytes 589832 | tf_op jit(solution)/shard_map/while/body/eval_jaxpr/ppermute | solution.py:19
  265.8 9.2 collective-permute-start.3
  267.2 9.6 collective-permute-start.2
  278.8 28.0 %collective-permute-start.3 = (bf16[2,6,64,128]{3,2,1,0:T(8,128)(2,1)S(1)}, bf16[2,6,64,128]{3,2,1,0:T(8,128)(2,1)}, u32[]{:S(2)}, u32[]{:S(2)}) collective-permute-start(bf16[2,6,64,128]{3,2,1,0:T(8,128)(2,1)S(1)} %convert_element_type.253), channel_id=1, source_target_pairs={{16,0},{32,16},{48,32},{64,48},{80,64},{96,80},{112,96},{128,112},... | collective-permute-start | bytes 589832 | tf_op jit(solution)/shard_map/while/body/eval_jaxpr/ppermute | solution.py:19
  280.2 28.3 %collective-permute-start.2 = (bf16[2,6,64,128]{3,2,1,0:T(8,128)(2,1)S(1)}, bf16[2,6,64,128]{3,2,1,0:T(8,128)(2,1)S(1)}, u32[]{:S(2)}, u32[]{:S(2)}) collective-permute-start(bf16[2,6,64,128]{3,2,1,0:T(8,128)(2,1)S(1)} %convert_element_type.250), channel_id=1, source_target_pairs={{0,16},{16,32},{32,48},{48,64},{64,80},{80,96},{96,112},{112,128},... | collective-permute-start | bytes 589832 | tf_op jit(solution)/shard_map/while/body/eval_jaxpr/ppermute | solution.py:19
  310.5 8.6 collective-permute-start.3
  311.9 9.0 collective-permute-start.2
  322.9 31.2 %collective-permute-start.3 = (bf16[2,6,64,128]{3,2,1,0:T(8,128)(2,1)S(1)}, bf16[2,6,64,128]{3,2,1,0:T(8,128)(2,1)}, u32[]{:S(2)}, u32[]{:S(2)}) collective-permute-start(bf16[2,6,64,128]{3,2,1,0:T(8,128)(2,1)S(1)} %convert_element_type.253), channel_id=1, source_target_pairs={{16,0},{32,16},{48,32},{64,48},{80,64},{96,80},{112,96},{128,112},... | collective-permute-start | bytes 589832 | tf_op jit(solution)/shard_map/while/body/eval_jaxpr/ppermute | solution.py:19
  324.3 31.6 %collective-permute-start.2 = (bf16[2,6,64,128]{3,2,1,0:T(8,128)(2,1)S(1)}, bf16[2,6,64,128]{3,2,1,0:T(8,128)(2,1)S(1)}, u32[]{:S(2)}, u32[]{:S(2)}) collective-permute-start(bf16[2,6,64,128]{3,2,1,0:T(8,128)(2,1)S(1)} %convert_element_type.250), channel_id=1, source_target_pairs={{0,16},{16,32},{32,48},{48,64},{64,80},{80,96},{96,112},{112,128},... | collective-permute-start | bytes 589832 | tf_op jit(solution)/shard_map/while/body/eval_jaxpr/ppermute | solution.py:19
  369.3 23.6 %collective-permute-start.3 = (bf16[2,6,64,128]{3,2,1,0:T(8,128)(2,1)S(1)}, bf16[2,6,64,128]{3,2,1,0:T(8,128)(2,1)}, u32[]{:S(2)}, u32[]{:S(2)}) collective-permute-start(bf16[2,6,64,128]{3,2,1,0:T(8,128)(2,1)S(1)} %convert_element_type.253), channel_id=1, source_target_pairs={{16,0},{32,16},{48,32},{64,48},{80,64},{96,80},{112,96},{128,112},... | collective-permute-start | bytes 589832 | tf_op jit(solution)/shard_map/while/body/eval_jaxpr/ppermute | solution.py:19
  370.7 23.9 %collective-permute-start.2 = (bf16[2,6,64,128]{3,2,1,0:T(8,128)(2,1)S(1)}, bf16[2,6,64,128]{3,2,1,0:T(8,128)(2,1)S(1)}, u32[]{:S(2)}, u32[]{:S(2)}) collective-permute-start(bf16[2,6,64,128]{3,2,1,0:T(8,128)(2,1)S(1)} %convert_element_type.250), channel_id=1, source_target_pairs={{0,16},{16,32},{32,48},{48,64},{64,80},{80,96},{96,112},{112,128},... | collective-permute-start | bytes 589832 | tf_op jit(solution)/shard_map/while/body/eval_jaxpr/ppermute | solution.py:19
  396.7 156.7 %collective-permute-start.3 = (bf16[2,6,64,128]{3,2,1,0:T(8,128)(2,1)S(1)}, bf16[2,6,64,128]{3,2,1,0:T(8,128)(2,1)}, u32[]{:S(2)}, u32[]{:S(2)}) collective-permute-start(bf16[2,6,64,128]{3,2,1,0:T(8,128)(2,1)S(1)} %convert_element_type.253), channel_id=1, source_target_pairs={{16,0},{32,16},{48,32},{64,48},{80,64},{96,80},{112,96},{128,112},... | collective-permute-start | bytes 589832 | tf_op jit(solution)/shard_map/while/body/eval_jaxpr/ppermute | solution.py:19
  398.0 157.1 %collective-permute-start.2 = (bf16[2,6,64,128]{3,2,1,0:T(8,128)(2,1)S(1)}, bf16[2,6,64,128]{3,2,1,0:T(8,128)(2,1)S(1)}, u32[]{:S(2)}, u32[]{:S(2)}) collective-permute-start(bf16[2,6,64,128]{3,2,1,0:T(8,128)(2,1)S(1)} %convert_element_type.250), channel_id=1, source_target_pairs={{0,16},{16,32},{32,48},{48,64},{64,80},{80,96},{96,112},{112,128},... | collective-permute-start | bytes 589832 | tf_op jit(solution)/shard_map/while/body/eval_jaxpr/ppermute | solution.py:19
  582.0 102.8 %all-gather.5.cloned.1.call-start = ((), (), s32[]{:S(2)}) async-start(), calls=%async_computation.3 | async-start | bytes 1327104 | tf_op jit(solution)/shard_map/all_gather | solution.py:138
  650.2 8.5 collective-permute-start.4
  659.4 634.4 %reduce-scatter.9.cloned.1.call-start = ((), (), s32[]{:S(2)}) async-start(), calls=%async_computation.5 | async-start | bytes 1769472
  718.8 23.1 %collective-permute-start.1 = (bf16[2,6,64,128]{3,2,1,0:T(8,128)(2,1)S(1)}, bf16[2,6,64,128]{3,2,1,0:T(8,128)(2,1)S(1)}, u32[]{:S(2)}, u32[]{:S(2)}) collective-permute-start(bf16[2,6,64,128]{3,2,1,0:T(8,128)(2,1)S(1)} %convert_element_type.260), channel_id=1, source_target_pairs={{16,0},{32,16},{48,32},{64,48},{80,64},{96,80},{112,96},{128,112},... | collective-permute-start | bytes 589832 | tf_op jit(solution)/shard_map/while/body/eval_jaxpr/ppermute | solution.py:19
  748.8 26.7 %collective-permute-start.1 = (bf16[2,6,64,128]{3,2,1,0:T(8,128)(2,1)S(1)}, bf16[2,6,64,128]{3,2,1,0:T(8,128)(2,1)S(1)}, u32[]{:S(2)}, u32[]{:S(2)}) collective-permute-start(bf16[2,6,64,128]{3,2,1,0:T(8,128)(2,1)S(1)} %convert_element_type.260), channel_id=1, source_target_pairs={{16,0},{32,16},{48,32},{64,48},{80,64},{96,80},{112,96},{128,112},... | collective-permute-start | bytes 589832 | tf_op jit(solution)/shard_map/while/body/eval_jaxpr/ppermute | solution.py:19
  750.1 29.4 %collective-permute-start = (bf16[2,6,64,128]{3,2,1,0:T(8,128)(2,1)S(1)}, bf16[2,6,64,128]{3,2,1,0:T(8,128)(2,1)S(1)}, u32[]{:S(2)}, u32[]{:S(2)}) collective-permute-start(bf16[2,6,64,128]{3,2,1,0:T(8,128)(2,1)S(1)} %convert_element_type.257), channel_id=1, source_target_pairs={{0,16},{16,32},{32,48},{48,64},{64,80},{80,96},{96,112},{112,128},... | collective-permute-start | bytes 589832 | tf_op jit(solution)/shard_map/while/body/eval_jaxpr/ppermute | solution.py:19
  793.1 27.8 %collective-permute-start.1 = (bf16[2,6,64,128]{3,2,1,0:T(8,128)(2,1)S(1)}, bf16[2,6,64,128]{3,2,1,0:T(8,128)(2,1)S(1)}, u32[]{:S(2)}, u32[]{:S(2)}) collective-permute-start(bf16[2,6,64,128]{3,2,1,0:T(8,128)(2,1)S(1)} %convert_element_type.260), channel_id=1, source_target_pairs={{16,0},{32,16},{48,32},{64,48},{80,64},{96,80},{112,96},{128,112},... | collective-permute-start | bytes 589832 | tf_op jit(solution)/shard_map/while/body/eval_jaxpr/ppermute | solution.py:19
  794.4 28.0 %collective-permute-start = (bf16[2,6,64,128]{3,2,1,0:T(8,128)(2,1)S(1)}, bf16[2,6,64,128]{3,2,1,0:T(8,128)(2,1)S(1)}, u32[]{:S(2)}, u32[]{:S(2)}) collective-permute-start(bf16[2,6,64,128]{3,2,1,0:T(8,128)(2,1)S(1)} %convert_element_type.257), channel_id=1, source_target_pairs={{0,16},{16,32},{32,48},{48,64},{64,80},{80,96},{96,112},{112,128},... | collective-permute-start | bytes 589832 | tf_op jit(solution)/shard_map/while/body/eval_jaxpr/ppermute | solution.py:19
  836.0 27.9 %collective-permute-start.1 = (bf16[2,6,64,128]{3,2,1,0:T(8,128)(2,1)S(1)}, bf16[2,6,64,128]{3,2,1,0:T(8,128)(2,1)S(1)}, u32[]{:S(2)}, u32[]{:S(2)}) collective-permute-start(bf16[2,6,64,128]{3,2,1,0:T(8,128)(2,1)S(1)} %convert_element_type.260), channel_id=1, source_target_pairs={{16,0},{32,16},{48,32},{64,48},{80,64},{96,80},{112,96},{128,112},... | collective-permute-start | bytes 589832 | tf_op jit(solution)/shard_map/while/body/eval_jaxpr/ppermute | solution.py:19
  837.3 28.0 %collective-permute-start = (bf16[2,6,64,128]{3,2,1,0:T(8,128)(2,1)S(1)}, bf16[2,6,64,128]{3,2,1,0:T(8,128)(2,1)S(1)}, u32[]{:S(2)}, u32[]{:S(2)}) collective-permute-start(bf16[2,6,64,128]{3,2,1,0:T(8,128)(2,1)S(1)} %convert_element_type.257), channel_id=1, source_target_pairs={{0,16},{16,32},{32,48},{48,64},{64,80},{80,96},{96,112},{112,128},... | collective-permute-start | bytes 589832 | tf_op jit(solution)/shard_map/while/body/eval_jaxpr/ppermute | solution.py:19
  878.9 29.1 %collective-permute-start.1 = (bf16[2,6,64,128]{3,2,1,0:T(8,128)(2,1)S(1)}, bf16[2,6,64,128]{3,2,1,0:T(8,128)(2,1)S(1)}, u32[]{:S(2)}, u32[]{:S(2)}) collective-permute-start(bf16[2,6,64,128]{3,2,1,0:T(8,128)(2,1)S(1)} %convert_element_type.260), channel_id=1, source_target_pairs={{16,0},{32,16},{48,32},{64,48},{80,64},{96,80},{112,96},{128,112},... | collective-permute-start | bytes 589832 | tf_op jit(solution)/shard_map/while/body/eval_jaxpr/ppermute | solution.py:19
  880.3 29.2 %collective-permute-start = (bf16[2,6,64,128]{3,2,1,0:T(8,128)(2,1)S(1)}, bf16[2,6,64,128]{3,2,1,0:T(8,128)(2,1)S(1)}, u32[]{:S(2)}, u32[]{:S(2)}) collective-permute-start(bf16[2,6,64,128]{3,2,1,0:T(8,128)(2,1)S(1)} %convert_element_type.257), channel_id=1, source_target_pairs={{0,16},{16,32},{32,48},{48,64},{64,80},{80,96},{96,112},{112,128},... | collective-permute-start | bytes 589832 | tf_op jit(solution)/shard_map/while/body/eval_jaxpr/ppermute | solution.py:19
  911.5 9.1 collective-permute-start.1
  912.9 9.3 collective-permute-start
  924.2 28.1 %collective-permute-start.1 = (bf16[2,6,64,128]{3,2,1,0:T(8,128)(2,1)S(1)}, bf16[2,6,64,128]{3,2,1,0:T(8,128)(2,1)S(1)}, u32[]{:S(2)}, u32[]{:S(2)}) collective-permute-start(bf16[2,6,64,128]{3,2,1,0:T(8,128)(2,1)S(1)} %convert_element_type.260), channel_id=1, source_target_pairs={{16,0},{32,16},{48,32},{64,48},{80,64},{96,80},{112,96},{128,112},... | collective-permute-start | bytes 589832 | tf_op jit(solution)/shard_map/while/body/eval_jaxpr/ppermute | solution.py:19
  925.6 28.6 %collective-permute-start = (bf16[2,6,64,128]{3,2,1,0:T(8,128)(2,1)S(1)}, bf16[2,6,64,128]{3,2,1,0:T(8,128)(2,1)S(1)}, u32[]{:S(2)}, u32[]{:S(2)}) collective-permute-start(bf16[2,6,64,128]{3,2,1,0:T(8,128)(2,1)S(1)} %convert_element_type.257), channel_id=1, source_target_pairs={{0,16},{16,32},{32,48},{48,64},{64,80},{80,96},{96,112},{112,128},... | collective-permute-start | bytes 589832 | tf_op jit(solution)/shard_map/while/body/eval_jaxpr/ppermute | solution.py:19
  956.2 8.6 collective-permute-start.1
  957.6 8.7 collective-permute-start
  968.4 32.6 %collective-permute-start.1 = (bf16[2,6,64,128]{3,2,1,0:T(8,128)(2,1)S(1)}, bf16[2,6,64,128]{3,2,1,0:T(8,128)(2,1)S(1)}, u32[]{:S(2)}, u32[]{:S(2)}) collective-permute-start(bf16[2,6,64,128]{3,2,1,0:T(8,128)(2,1)S(1)} %convert_element_type.260), channel_id=1, source_target_pairs={{16,0},{32,16},{48,32},{64,48},{80,64},{96,80},{112,96},{128,112},... | collective-permute-start | bytes 589832 | tf_op jit(solution)/shard_map/while/body/eval_jaxpr/ppermute | solution.py:19
  969.7 32.5 %collective-permute-start = (bf16[2,6,64,128]{3,2,1,0:T(8,128)(2,1)S(1)}, bf16[2,6,64,128]{3,2,1,0:T(8,128)(2,1)S(1)}, u32[]{:S(2)}, u32[]{:S(2)}) collective-permute-start(bf16[2,6,64,128]{3,2,1,0:T(8,128)(2,1)S(1)} %convert_element_type.257), channel_id=1, source_target_pairs={{0,16},{16,32},{32,48},{48,64},{64,80},{80,96},{96,112},{112,128},... | collective-permute-start | bytes 589832 | tf_op jit(solution)/shard_map/while/body/eval_jaxpr/ppermute | solution.py:19
  1015.8 22.2 %collective-permute-start.1 = (bf16[2,6,64,128]{3,2,1,0:T(8,128)(2,1)S(1)}, bf16[2,6,64,128]{3,2,1,0:T(8,128)(2,1)S(1)}, u32[]{:S(2)}, u32[]{:S(2)}) collective-permute-start(bf16[2,6,64,128]{3,2,1,0:T(8,128)(2,1)S(1)} %convert_element_type.260), channel_id=1, source_target_pairs={{16,0},{32,16},{48,32},{64,48},{80,64},{96,80},{112,96},{128,112},... | collective-permute-start | bytes 589832 | tf_op jit(solution)/shard_map/while/body/eval_jaxpr/ppermute | solution.py:19
  1017.1 22.3 %collective-permute-start = (bf16[2,6,64,128]{3,2,1,0:T(8,128)(2,1)S(1)}, bf16[2,6,64,128]{3,2,1,0:T(8,128)(2,1)S(1)}, u32[]{:S(2)}, u32[]{:S(2)}) collective-permute-start(bf16[2,6,64,128]{3,2,1,0:T(8,128)(2,1)S(1)} %convert_element_type.257), channel_id=1, source_target_pairs={{0,16},{16,32},{32,48},{48,64},{64,80},{80,96},{96,112},{112,128},... | collective-permute-start | bytes 589832 | tf_op jit(solution)/shard_map/while/body/eval_jaxpr/ppermute | solution.py:19
  1041.5 156.6 %collective-permute-start.1 = (bf16[2,6,64,128]{3,2,1,0:T(8,128)(2,1)S(1)}, bf16[2,6,64,128]{3,2,1,0:T(8,128)(2,1)S(1)}, u32[]{:S(2)}, u32[]{:S(2)}) collective-permute-start(bf16[2,6,64,128]{3,2,1,0:T(8,128)(2,1)S(1)} %convert_element_type.260), channel_id=1, source_target_pairs={{16,0},{32,16},{48,32},{64,48},{80,64},{96,80},{112,96},{128,112},... | collective-permute-start | bytes 589832 | tf_op jit(solution)/shard_map/while/body/eval_jaxpr/ppermute | solution.py:19
  1042.9 156.8 %collective-permute-start = (bf16[2,6,64,128]{3,2,1,0:T(8,128)(2,1)S(1)}, bf16[2,6,64,128]{3,2,1,0:T(8,128)(2,1)S(1)}, u32[]{:S(2)}, u32[]{:S(2)}) collective-permute-start(bf16[2,6,64,128]{3,2,1,0:T(8,128)(2,1)S(1)} %convert_element_type.257), channel_id=1, source_target_pairs={{0,16},{16,32},{32,48},{48,64},{64,80},{80,96},{96,112},{112,128},... | collective-permute-start | bytes 589832 | tf_op jit(solution)/shard_map/while/body/eval_jaxpr/ppermute | solution.py:19
  (76 other events, 839.4 us)
Sparse Core Ops, SparseCore 0:
  9.2 29.1 all-gather.2
  582.1 65.3 reduce-scatter.6
  659.5 25.2 all-gather.4
  1226.4 67.4 reduce-scatter.8
where the time goes:
time: 1320 us; the launch traced here: 1300 us
  starting transfers between devices  758 us (57%)
  waiting for transfers between devices  263 us (20%)
  other arithmetic  121 us (9%)
  matrix products  80.8 us (6%)
  local copies, waits for them, and re-layouts  60.1 us (5%)
  between operations  14.3 us (1%)
    ppermute x61, starting transfers between devices, from_behind(): return lax.ppermute(block, axis, route)  757 us
    unnamed x6, waiting for transfers between devices  134 us
    ppermute x61, waiting for transfers between devices, from_behind(): return lax.ppermute(block, axis, route)  76.8 us
    all_gather x2, waiting for transfers between devices, layer(): lax.all_gather(hidden, 'head', axis=1, tiled=True)  52.5 us
    convert_element_type x30, other arithmetic, hop(): from_behind(backward[0].astype(jnp.bfloat16), 'seg', -1).astype(jnp.float32)  37.6 us
    select_n x32, other arithmetic, advance(): state = jnp.where(lag == 0, begin, received)  36.9 us
  transfers between devices with their start and end apart: 65, of which 48 were waited for; matrix products, arithmetic and copies ran while one was open for 6% of the time, Pallas kernels for 0%

commit v1 on v0

v1 whole, which is shorter than its diff:
```python
import functools
import math

import jax
import jax.numpy as jnp
from jax import lax
from jax.experimental import pallas as pl
from jax.experimental.pallas import tpu as pltpu
from jax.sharding import PartitionSpec as P

MB = 64
C1 = math.sqrt(2.0 / math.pi)
C3 = 0.044715
f32 = jnp.float32
bf = jnp.bfloat16


def dot(a, b):
    return lax.dot_general(a, b, (((1,), (0,)), ((), ())), preferred_element_type=f32)


def dot_nt(a, b):
    return lax.dot_general(a, b, (((1,), (1,)), ((), ())), preferred_element_type=f32)


def dot_tn(a, b):
    return lax.dot_general(a, b, (((0,), (0,)), ((), ())), preferred_element_type=f32)


def smooth(z):
    t = jnp.tanh(z * (C1 + (C1 * C3) * (z * z)))
    h = 0.5 * z
    return h + h * t


def smooth_slope(z):
    z2 = z * z
    t = jnp.tanh(z * (C1 + (C1 * C3) * z2))
    h = 0.5 * z
    return h + h * t, 0.5 + 0.5 * t + h * (1.0 - t * t) * (C1 + (3.0 * C1 * C3) * z2)


def chain_kernel(nb, q, k, v, km, scale, u0, w0, o, u, w):
    u[...] = u0[...]
    w[...] = w0[...]

    def step(b, z):
        kb, kn, kmb, qb = k[b], k[jnp.minimum(b + 1, nb - 1)], km[b], q[b]
        a, s = smooth_slope(z)
        ab = a.astype(bf)
        wb = w[...].astype(bf)
        e = (kb.astype(f32) - v[b].astype(f32)) + dot_nt(ab, wb)
        back = (dot(e.astype(bf), wb) * s).astype(bf)
        ahead = dot(kn, u[...].astype(bf))
        gram = dot_nt(kn, kmb).astype(bf)
        z_next = ahead - dot(gram, back)
        un = u[...] - dot_tn(kmb, back)
        u[...] = un
        wn = w[...] - dot_tn((e * scale[b]).astype(bf), ab)
        w[...] = wn
        lifted = smooth(dot(qb, un.astype(bf))).astype(bf)
        o[b] = qb.astype(f32) + dot_nt(lifted, wn.astype(bf))
        return z_next

    lax.fori_loop(0, nb, step, dot(k[0], u0[...].astype(bf)))


def run_chain(q, k, v, km, scale, u0, w0):
    nb = q.shape[0]
    vm = pl.BlockSpec(memory_space=pltpu.VMEM)
    return pl.pallas_call(
        functools.partial(chain_kernel, nb),
        out_shape=jax.ShapeDtypeStruct(q.shape, f32),
        in_specs=[vm] * 7,
        out_specs=vm,
        scratch_shapes=[pltpu.VMEM(u0.shape, f32), pltpu.VMEM(w0.shape, f32)],
        compiler_params=pltpu.CompilerParams(vmem_limit_bytes=40 << 20),
        name="chain",
    )(q, k, v, km, scale, u0, w0)


def rescale(rows):
    return rows * lax.rsqrt(jnp.mean(rows * rows, axis=-1, keepdims=True) + 1e-06)


def layer(hidden, weights):
    in_w, out_rows, expand, contract, rates, live = weights
    n_seg = lax.axis_size("seg")
    heads, width = expand.shape[1], expand.shape[2]
    rows = hidden.shape[0]
    projected = jnp.einsum(
        "td,jdc->tjc",
        lax.all_gather(hidden, "head", axis=1, tiled=True),
        in_w,
        preferred_element_type=f32,
    )
    rounded = lax.optimization_barrier(projected.astype(bf)).astype(f32)
    unit = rescale(rounded.reshape(rows, 3, heads, width)).astype(bf)
    pieces = jnp.transpose(unit, (2, 0, 1, 3)).reshape(heads, rows, 3 * width)
    pieces = jnp.repeat(pieces, 2, axis=0)
    pieces = jnp.concatenate([pieces, pieces[: n_seg - 2 * heads]], axis=0)
    got = lax.all_to_all(pieces, "seg", 0, 0, tiled=True)
    blocks = n_seg * rows // MB
    me = lax.rem(lax.axis_index("seg"), 2 * heads)
    head, way = me // 2, lax.rem(me, 2)
    got = got.reshape(blocks, MB, 3 * width)
    mask = live.reshape(blocks, MB, 1)
    got = jnp.where(way == 1, got[::-1], got)
    mask = jnp.where(way == 1, mask[::-1], mask)
    q, k, v = got[..., :width], got[..., width : 2 * width], got[..., 2 * width :]
    scale = mask * (rates[way, head] / (width * MB))
    km = (k.astype(f32) * scale).astype(bf)
    out = run_chain(
        q,
        k,
        v,
        km,
        jnp.broadcast_to(scale, q.shape),
        expand[way, head],
        jnp.swapaxes(contract[way, head], 0, 1),
    )
    out = jnp.where(way == 1, out[::-1], out).astype(bf)
    back = lax.all_to_all(out.reshape(n_seg, rows, width), "seg", 0, 0, tiled=True)
    back = back[: 2 * heads].reshape(heads, 2, rows, width).astype(f32)
    mixture = jnp.swapaxes(back[:, 0] + back[:, 1], 0, 1).reshape(rows, heads * width).astype(bf)
    term = jnp.dot(mixture, out_rows, preferred_element_type=f32)
    summed = lax.psum_scatter(term.astype(bf), "head", scatter_dimension=1, tiled=True).astype(f32)
    return (hidden.astype(f32) + summed).astype(bf)


def local(tokens, in_weight, out_weight, expand_init, contract_init, inner_rate, seg_counts):
    counts = lax.all_gather(seg_counts, "seg", axis=0, tiled=True)
    position = lax.broadcasted_iota(jnp.int32, (counts.shape[0], tokens.shape[0]), 1)
    live = (position < counts[:, None]).astype(f32)
    weights = (in_weight[0], out_weight[0], expand_init[0], contract_init[0], inner_rate[0], live)
    earlier = layer(tokens, weights)
    n = lax.axis_size("section")
    handed = lax.ppermute(earlier, "section", [(i, i + 1) for i in range(n - 1)])
    later = layer(handed, weights)
    panel = jnp.where(lax.axis_index("section") == 0, earlier, later)
    return panel[None]


def solution(mesh):
    placed = (
        P("seg", "head"),
        P("section", None, None, "head"),
        P("section", "head", None),
        P("section", None, "head", None, None),
        P("section", None, "head", None, None),
        P("section", None, "head"),
        P("seg"),
    )
    return jax.shard_map(
        local, mesh=mesh, in_specs=placed, out_specs=P("section", "seg", "head"), check_vma=False
    )
```

time: 1320 us -> 393 us (0.30); the launches traced: 1300 us -> 392 us
  starting transfers between devices: 758 us -> 9.31 us
  waiting for transfers between devices: 263 us -> 129 us
  blocking collectives: 0 us -> 130 us
  other arithmetic: 121 us -> 10.9 us
  matrix products: 80.8 us -> 13.6 us
  Pallas kernels: 0 us -> 62.2 us
  local copies, waits for them, and re-layouts: 60.1 us -> 22.8 us
    ppermute x61 -> x1, starting transfers between devices: 757 us -> 1.28 us  [local(): lax.ppermute(earlier, 'section', [(i, i + 1) for i in range(n - 1)])]
    all_to_all x0 -> x3, blocking collectives: none -> 83.9 us  [the longest x1 45.9 us: layer(): got = lax.all_to_all(pieces, 'seg', 0, 0, tiled=True)]
    ppermute x61 -> x1, waiting for transfers between devices: 76.8 us -> 7.24 us  [local(): lax.ppermute(earlier, 'section', [(i, i + 1) for i in range(n - 1)])]
    unnamed x6, waiting for transfers between devices: 134 us -> 65.6 us
    dot_general x88 -> x4, matrix products: 80.8 us -> 13.6 us  [the longest x2 11 us: layer(): jnp.einsum('td,jdc->tjc', lax.all_gather(hidden, 'head', axis=1, tiled=Tr...]
    pallas_call x0 -> x2, Pallas kernels: none -> 62.2 us  [run_chain(): pl.pallas_call(functools.partial(chain_kernel, nb), out_shape=jax.ShapeDt...]
    convert_element_type x154 -> x10, other arithmetic: 63.4 us -> 2.12 us  [the longest x2 1.36 us: layer(): km = (k.astype(f32) * scale).astype(bf)]
    unnamed x0 -> x1, blocking collectives: none -> 45.8 us
  transfers between devices with their start and end apart: 65 -> 6, of which waited for: 48 -> 5; matrix products, arithmetic and copies ran while one was open for 6% -> 1% of each run, Pallas kernels for 0% -> 0%
where the time goes in v1:
time: 393 us; the launch traced here: 392 us
  blocking collectives  130 us (33%)
  waiting for transfers between devices  129 us (33%)
  Pallas kernels  62.2 us (16%)
  local copies, waits for them, and re-layouts  22.8 us (6%)
  between operations  14.2 us (4%)
  matrix products  13.6 us (3%)
  other arithmetic  10.9 us (3%)
  starting transfers between devices  9.31 us (2%)
    unnamed x6, waiting for transfers between devices  65.6 us
    pallas_call x2, Pallas kernels, run_chain(): pl.pallas_call(functools.partial(chain_kernel, nb), out_shape=jax.ShapeDt...  62.2 us
    all_gather x2, waiting for transfers between devices, layer(): lax.all_gather(hidden, 'head', axis=1, tiled=True)  56.5 us
    all_to_all x1, blocking collectives, layer(): got = lax.all_to_all(pieces, 'seg', 0, 0, tiled=True)  45.9 us
    unnamed x1, blocking collectives  45.8 us
    all_to_all x2, blocking collectives, layer(): lax.all_to_all(out.reshape(n_seg, rows, width), 'seg', 0, 0, tiled=True)  38.1 us
    dot_general x2, matrix products, layer(): jnp.einsum('td,jdc->tjc', lax.all_gather(hidden, 'head', axis=1, tiled=Tr...  11 us
    unnamed x29, local copies, waits for them, and re-layouts  9.7 us
  transfers between devices with their start and end apart: 6, of which 5 were waited for; matrix products, arithmetic and copies ran while one was open for 1% of the time, Pallas kernels for 0%

profile of v1, /device:TPU:4, one launch (start us, length us, event | category | flops | bytes accessed | tf_op | source)
XLA Modules:
  0.0 392.2 jit_solution(8094949185531212499)
XLA Ops:
  6.5 0.7 all-gather.3.cloned.1.call-update
  7.3 31.1 %all-gather.3.cloned.1.call-done = bf16[192,3072]{1,0:T(8,128)(2,1)} async-done(((bf16[192,384]{1,0:T(8,128)(2,1)}), bf16[192,3072]{1,0:T(8,128)(2,1)}) %all-gather.3.cloned.1.call-update) | async-done | bytes 1179664 | tf_op jit(solution)/shard_map/all_gather | solution.py:93
  38.4 5.9 %fusion.8 = bf16[192,3,384]{2,0,1:T(8,128)(2,1)} fusion(bf16[1,3,3072,384]{3,2,1,0:T(8,128)(2,1)} %param.8, bf16[192,3072]{1,0:T(8,128)(2,1)} %all-gather.3.cloned.1.call-done), kind=kOutput, calls=%fused_computation.18 | convolution fusion | flops 1359175680 | bytes 8699904 | tf_op jit(solution)/shard_map/td,jdc->tjc/dot_general | solution.py:91
  44.3 1.2 copy.30
  45.9 0.7 slice.74
  46.9 0.9 copy.33
  48.1 1.4 pad_maximum_fusion
  49.5 7.9 %all-to-all-start = ((bf16[16,192,192]{2,1,0:T(8,128)(2,1)}), bf16[16,192,192]{2,1,0:T(8,128)(2,1)}, u32[]{:S(2)}, u32[]{:S(2)}) async-start(bf16[16,192,192]{2,1,0:T(8,128)(2,1)} %pad_maximum_fusion), calls=%async_computation | async-start | bytes 3145728 | tf_op jit(solution)/shard_map/all_to_all | solution.py:102
  58.2 0.6 dynamic-slice.3
  58.8 0.8 dynamic-update-slice
  59.5 45.8 %all-reduce = s32[16]{0:T(128)S(1)} all-reduce(s32[16]{0:T(128)S(1)} %dynamic-update-slice), channel_id=1, replica_groups=mesh['seg'=16,'head'=8,'section'=2] {'seg'}, use_global_device_ids=true, to_apply=%add | all-reduce | flops 16 | bytes 128
  105.7 0.6 fusion.24
  106.2 0.8 dynamic-slice_bitcast_fusion.1.u0
  107.0 0.8 dynamic-slice_bitcast_fusion.w0
  107.8 0.7 multiply_bitcast_fusion
  108.5 2.7 reverse_select_fusion.3
  111.2 0.7 fusion.23
  111.8 0.7 multiply_convert_fusion.1.km
  113.0 31.1 %chain.2 = f32[48,64,64]{2,1,0:T(8,128)S(1)} custom-call(bf16[48,64,64]{2,1,0:T(8,128)(2,1)S(1)} %get-tuple-element.10.q, bf16[48,64,64]{2,1,0:T(8,128)(2,1)S(1)} %get-tuple-element.9.k, bf16[48,64,64]{2,1,0:T(8,128)(2,1)S(1)} %get-tuple-element.8.v, bf16[48,64,64]{2,1,0:T(8,128)(2,1)S(1)} %multiply_convert_fusion.1.km, f32[48,64,64]{2,1,0:T(8,128)S(1)} %mul.52.scale, ...), custom_call_target="tpu_custom_call" | custom-call | tf_op jit(solution)/shard_map/chain/pallas_call | solution.py:71
  144.3 1.1 copy.35
  145.5 17.6 %all_to_all.20 = bf16[16,192,64]{1,2,0:T(8,128)(2,1)S(1)} all-to-all(bf16[16,192,64]{1,2,0:T(8,128)(2,1)} %copy.35), channel_id=1, replica_groups=mesh['seg'=16,'head'=8,'section'=2] {'seg'}, dimensions={0} | all-to-all | bytes 786432 | tf_op jit(solution)/shard_map/all_to_all | solution.py:123
  163.3 1.8 convolution_convert_fusion.1
  165.1 2.5 copy.42
  167.7 32.1 %reduce-scatter.7.cloned.1.call-done = bf16[384,192]{1,0:T(8,128)(2,1)} async-done(((bf16[3072,192]{1,0:T(8,128)(2,1)}), bf16[384,192]{1,0:T(8,128)(2,1)}) %reduce-scatter.7.cloned.1.call-update) | async-done | bytes 147472
  199.8 1.1 copy.43
  201.0 0.7 copy-done.5
  201.6 1.3 collective-permute-start
  202.9 7.2 %collective-permute-done = bf16[192,384]{1,0:T(8,128)(2,1)S(1)} collective-permute-done((bf16[192,384]{1,0:T(8,128)(2,1)S(1)}, bf16[192,384]{1,0:T(8,128)(2,1)S(1)}, u32[]{:S(2)}, u32[]{:S(2)}) %collective-permute-start) | collective-permute-done | bytes 147488 | tf_op jit(solution)/shard_map/ppermute | solution.py:138
  210.1 0.7 copy-done.7
  210.9 25.4 %all-gather.5.cloned.1.call-done = bf16[192,3072]{1,0:T(8,128)(2,1)} async-done(((bf16[192,384]{1,0:T(8,128)(2,1)}), bf16[192,3072]{1,0:T(8,128)(2,1)}) %all-gather.5.cloned.1.call-update) | async-done | bytes 1179664 | tf_op jit(solution)/shard_map/all_gather | solution.py:93
  236.2 5.1 %fusion.11 = bf16[192,3,384]{2,0,1:T(8,128)(2,1)S(1)} fusion(bf16[1,3,3072,384]{3,2,1,0:T(8,128)(2,1)} %param.8, bf16[192,3072]{1,0:T(8,128)(2,1)} %all-gather.5.cloned.1.call-done), kind=kOutput, calls=%fused_computation.19 | convolution fusion | flops 1359175680 | bytes 8699904 | tf_op jit(solution)/shard_map/td,jdc->tjc/dot_general | solution.py:91
  241.3 1.3 copy.36
  242.6 1.5 multiply_reduce_fusion
  244.4 0.9 copy.37
  245.3 1.3 copy.38
  247.2 45.9 %all_to_all.21 = bf16[16,192,192]{2,1,0:T(8,128)(2,1)S(1)} all-to-all(bf16[16,192,192]{2,1,0:T(8,128)(2,1)S(1)} %pad_maximum_fusion.1), channel_id=1, replica_groups=mesh['seg'=16,'head'=8,'section'=2] {'seg'}, dimensions={0} | all-to-all | bytes 2359296 | tf_op jit(solution)/shard_map/all_to_all | solution.py:102
  293.1 0.5 reverse_select_fusion.1
  293.6 0.7 multiply_convert_fusion.km
  294.3 0.7 fusion.22
  295.0 0.7 copy-done.2
  295.7 31.1 %chain.3 = f32[48,64,64]{2,1,0:T(8,128)S(1)} custom-call(bf16[48,64,64]{2,1,0:T(8,128)(2,1)S(1)} %get-tuple-element.7.q, bf16[48,64,64]{2,1,0:T(8,128)(2,1)S(1)} %get-tuple-element.6.k, bf16[48,64,64]{2,1,0:T(8,128)(2,1)S(1)} %get-tuple-element.5.v, bf16[48,64,64]{2,1,0:T(8,128)(2,1)S(1)} %multiply_convert_fusion.km, f32[48,64,64]{2,1,0:T(8,128)S(1)} %copy-done.2, ...), custom_call_target="tpu_custom_call" | custom-call | tf_op jit(solution)/shard_map/chain/pallas_call | solution.py:71
  327.0 1.1 copy.41
  328.1 20.4 %all_to_all.22 = bf16[16,192,64]{1,2,0:T(8,128)(2,1)S(1)} all-to-all(bf16[16,192,64]{1,2,0:T(8,128)(2,1)} %copy.41), channel_id=1, replica_groups=mesh['seg'=16,'head'=8,'section'=2] {'seg'}, dimensions={0} | all-to-all | bytes 786432 | tf_op jit(solution)/shard_map/all_to_all | solution.py:123
  348.7 0.8 convolution_convert_fusion
  349.5 1.6 copy.44
  351.2 32.7 %reduce-scatter.9.cloned.1.call-done = bf16[384,192]{1,0:T(8,128)(2,1)} async-done(((bf16[3072,192]{1,0:T(8,128)(2,1)}), bf16[384,192]{1,0:T(8,128)(2,1)}) %reduce-scatter.9.cloned.1.call-update) | async-done | bytes 147472
  383.9 1.1 copy.45
  385.0 0.7 fusion.21
  (61 shorter events, 3.4 us)
Async XLA Ops:
  6.5 156.7 %copy-start = (bf16[1,384,3072]{2,1,0:T(8,128)(2,1)S(1)}, bf16[1,384,3072]{2,1,0:T(8,128)(2,1)}, u32[]{:S(2)}) copy-start(bf16[1,384,3072]{2,1,0:T(8,128)(2,1)} %param.9) | copy-start | bytes 7077892
  6.5 31.9 %all-gather.3.cloned.1.call-start = ((), (), s32[]{:S(2)}) async-start(), calls=%async_computation.6 | async-start | bytes 1327104 | tf_op jit(solution)/shard_map/all_gather | solution.py:93
  49.5 8.7 %copy-start.10 = (u32[256]{0:T(256)S(1)}, u32[256]{0:T(256)}, u32[]{:S(2)}) copy-start(u32[256]{0:T(256)} %constant.57) | copy-start | bytes 3076
  49.5 56.1 %copy-start.9 = (f32[1,2,6]{2,1,0:T(2,128)S(1)}, f32[1,2,6]{2,1,0:T(2,128)}, u32[]{:S(2)}) copy-start(f32[1,2,6]{2,1,0:T(2,128)} %param.12) | copy-start | bytes 148
  49.5 59.0 %all-to-all-start = ((bf16[16,192,192]{2,1,0:T(8,128)(2,1)}), bf16[16,192,192]{2,1,0:T(8,128)(2,1)}, u32[]{:S(2)}, u32[]{:S(2)}) async-start(bf16[16,192,192]{2,1,0:T(8,128)(2,1)} %pad_maximum_fusion), calls=%async_computation | async-start | bytes 3145728 | tf_op jit(solution)/shard_map/all_to_all | solution.py:102
  57.4 142.4 %reduce-scatter.7.cloned.1.call-start = ((), (), s32[]{:S(2)}) async-start(), calls=%async_computation.8 | async-start | bytes 1769472
  113.0 31.1 %copy-start.1 = (f32[48,64,64]{2,1,0:T(8,128)}, f32[48,64,64]{2,1,0:T(8,128)S(1)}, u32[]{:S(2)}) copy-start(f32[48,64,64]{2,1,0:T(8,128)S(1)} %mul.52.scale) | copy-start | bytes 2359300
  167.6 33.3 %copy-start.4 = (bf16[192,384]{1,0:T(8,128)(2,1)S(1)}, bf16[192,384]{1,0:T(8,128)(2,1)}, u32[]{:S(2)}) copy-start(bf16[192,384]{1,0:T(8,128)(2,1)} %param.7) | copy-start | bytes 442372
  167.7 68.6 %all-gather.5.cloned.1.call-start = ((), (), s32[]{:S(2)}) async-start(), calls=%async_computation.7 | async-start | bytes 1327104 | tf_op jit(solution)/shard_map/all_gather | solution.py:93
  200.9 0.7 copy-start.5
  201.6 8.5 %collective-permute-start = (bf16[192,384]{1,0:T(8,128)(2,1)S(1)}, bf16[192,384]{1,0:T(8,128)(2,1)S(1)}, u32[]{:S(2)}, u32[]{:S(2)}) collective-permute-start(bf16[192,384]{1,0:T(8,128)(2,1)S(1)} %add_convert_fusion.1), channel_id=1, source_target_pairs={{0,1},{2,3},{4,5},{6,7},{8,9},{10,11},{12,13},{14,15},{16,17},{18,... | collective-permute-start | bytes 442376 | tf_op jit(solution)/shard_map/ppermute | solution.py:138
  210.1 0.7 copy-start.7
  210.8 173.1 %reduce-scatter.9.cloned.1.call-start = ((), (), s32[]{:S(2)}) async-start(), calls=%async_computation.9 | async-start | bytes 1769472
  242.6 1.6 copy-start.3
  294.3 1.4 copy-start.2
  351.1 33.8 %copy-start.6 = (bf16[192,384]{1,0:T(8,128)(2,1)S(1)}, bf16[192,384]{1,0:T(8,128)(2,1)}, u32[]{:S(2)}) copy-start(bf16[192,384]{1,0:T(8,128)(2,1)} %copy-done.5) | copy-start | bytes 442372
  351.1 33.8 %copy-start.8 = (bf16[192,384]{1,0:T(8,128)(2,1)S(1)}, bf16[192,384]{1,0:T(8,128)(2,1)}, u32[]{:S(2)}) copy-start(bf16[192,384]{1,0:T(8,128)(2,1)} %copy-done.7) | copy-start | bytes 442372
Sparse Core Ops, SparseCore 0:
  9.2 29.1 all-gather.2
  167.8 31.9 reduce-scatter.6
  210.9 25.2 all-gather.4
  351.3 32.5 reduce-scatter.8

commit v2 on v1

v2 whole, which is shorter than its diff:
```python
import functools
import math

import jax
import jax.numpy as jnp
from jax import lax
from jax.experimental import pallas as pl
from jax.experimental.pallas import tpu as pltpu
from jax.sharding import PartitionSpec as P

MB = 64
C1 = math.sqrt(2.0 / math.pi)
C3 = 0.044715
f32 = jnp.float32
bf = jnp.bfloat16


def dot(a, b):
    return lax.dot_general(a, b, (((1,), (0,)), ((), ())), preferred_element_type=f32)


def dot_nt(a, b):
    return lax.dot_general(a, b, (((1,), (1,)), ((), ())), preferred_element_type=f32)


def dot_tn(a, b):
    return lax.dot_general(a, b, (((0,), (0,)), ((), ())), preferred_element_type=f32)


def smooth(z):
    t = jnp.tanh(z * (C1 + (C1 * C3) * (z * z)))
    h = 0.5 * z
    return h + h * t


def smooth_slope(z):
    z2 = z * z
    t = jnp.tanh(z * (C1 + (C1 * C3) * z2))
    h = 0.5 * z
    return h + h * t, 0.5 + 0.5 * t + h * (1.0 - t * t) * (C1 + (3.0 * C1 * C3) * z2)


def chain_step(xl, bp, b, bn, z, bk, sc, u, w, ub, wk):
    xp, xb, xn = xl[bp, 0:64], xl[b, 0:64], xl[bn, 0:64]
    dp = xl[b, 64:96].astype(f32)
    hi = lax.broadcasted_iota(jnp.int32, (64, 128), 1) >= 64
    a, s = smooth_slope(z)
    s = s * sc
    ab = a.astype(bf)
    wkv = wk[...]
    p = dot_nt(ab, wkv)
    un = u[...] - dot_tn(xp, bk)[64:128]
    u[...] = un
    ub[64:128] = un.astype(bf)
    zu = dot(xn, ub[0:128])
    zq = dot(xp, ub[64:192])
    delta = jnp.where(hi, jnp.concatenate([pltpu.roll(dp, 64, 1), dp], 0), 0.0)
    e = delta + p
    f = dot(e.astype(bf), wkv)
    back = (f * s).astype(bf)
    gram = dot_nt(jnp.where(hi, xn, jnp.zeros_like(xn)), xb).astype(bf)
    zn = zu - dot(gram, back)
    aq = smooth(zq).astype(bf)
    out = pltpu.roll(xp.astype(f32), 64, 1) + dot_nt(aq, wkv)
    wn = w[...] - dot_tn((e * sc).astype(bf), ab)[64:128]
    w[...] = wn
    wk[64:128] = wn.astype(bf)
    return zn, back, out


def kernel(
    n_seg, n_head, heads,
    tokens, in_w, out_w, expand, contract, rate, counts,
    panel,
    inw, outw, hbuf, stg, xl, ini_s, ini, craw, exs, exl, mxs, mixb,
    p1, p2f, rs1, p2, rs2, u, w, ub, wk,
    wsem, tsem, isem, ag_s, ag_r, hop_s, hop_r, push_s, ch_r, fw_s, ex_s, ex_r,
    mix_s, mix_r, rs1_s, rs1_r, rs2_s, rs2_r, ini_ss, ini_r,
):
    rows = tokens.shape[0]
    cols = tokens.shape[1]
    chunks = rows // MB
    nb = n_seg * chunks
    half = nb // 2
    n_y = n_head // 2
    units = 2 * heads
    first = (n_seg - units) // 2
    sec = lax.axis_index("section")
    seg = lax.axis_index("seg")
    hd = lax.axis_index("head")
    y = hd // 2
    c = lax.rem(hd, 2)
    sib = 2 * y + 1 - c
    far = 1 - sec
    late = seg // (n_seg // 2)
    in_chain = jnp.logical_and(seg >= first, seg < first + units)
    unit = seg - first
    cg = unit // heads
    mine = unit - cg * heads
    holder = jnp.logical_and(in_chain, cg == c)

    def dev(s, h, x):
        return {"seg": s, "head": h, "section": x}

    def send(src, dst, s_sem, r_sem, device):
        return pltpu.make_async_remote_copy(
            src_ref=src, dst_ref=dst, send_sem=s_sem, recv_sem=r_sem,
            device_id=device, device_id_type=pl.DeviceIdType.MESH,
        )

    def span(ct):
        return pl.ds(pl.multiple_of(ct * MB, MB), MB)

    load_in = pltpu.make_async_copy(in_w.at[0], inw, wsem.at[0])
    load_out = pltpu.make_async_copy(out_w.at[0], outw, wsem.at[1])
    load_tok = pltpu.make_async_copy(tokens, hbuf.at[hd], tsem)

    @pl.when(sec == 0)
    def _():
        load_tok.start()

    load_in.start()
    load_out.start()

    barrier = pltpu.get_barrier_semaphore()

    def greet(device):
        pl.semaphore_signal(barrier, inc=1, device_id=device, device_id_type=pl.DeviceIdType.MESH)

    for k in range(1, n_head):
        greet(dev(seg, lax.rem(hd + k, n_head), sec))

    @pl.when(sec == 1)
    def _():
        greet(dev(seg, hd, 0))

    for j in range(heads):
        greet(dev(heads * c + j + first, 2 * y + 1 - late, far))

    @pl.when(in_chain)
    def _():
        for k in range(n_seg // 2):
            greet(dev(c * (n_seg // 2) + k, 2 * y + cg, far))
        greet(dev(seg, 2 * y + cg, far))

    total = n_head - 1 + heads + (1 - sec)
    total = total + jnp.where(in_chain, n_seg // 2, 0) + jnp.where(holder, 2, 0)
    pl.semaphore_wait(barrier, total)

    def direct(ct, k):
        to = jnp.int32(sib) if k == 0 else 2 * lax.rem(y + k, n_y) + c
        part = hbuf.at[hd, span(ct)]
        return send(part, part, ag_s.at[k, ct], ag_r.at[hd, ct], dev(seg, to, sec))

    def pass_on(ct, k):
        slot = 2 * lax.rem(y + k, n_y) + c
        part = hbuf.at[slot, span(ct)]
        return send(part, part, ag_s.at[n_y - 1 + k, ct], ag_r.at[slot, ct], dev(seg, sib, sec))

    def hop(ct):
        return send(panel.at[0, span(ct)], hbuf.at[hd, span(ct)], hop_s.at[ct], hop_r.at[ct], dev(seg, hd, 1))

    def arrived(slot, ct):
        part = hbuf.at[slot, span(ct)]
        send(part, part, ag_s.at[0, ct], ag_r.at[slot, ct], dev(seg, sib, sec)).wait_recv()

    flip = lax.rem(late + sec, 2)

    def need_order(t):
        return t + flip * (chunks - 1 - 2 * t)

    def done_order(t):
        return t + (1 - late) * (chunks - 1 - 2 * t)

    @pl.when(sec == 0)
    def _():
        load_tok.wait()

        def go(t, _):
            for k in (1, 3, 2, 0):
                direct(need_order(t), k).start()
            return 0

        lax.fori_loop(0, chunks, go, 0)

    def init_send(way):
        return send(ini_s.at[way], ini, ini_ss.at[way], ini_r, dev(seg, 2 * y + way, far))

    @pl.when(holder)
    def _():
        loads = []
        for way in range(2):
            loads.append(pltpu.make_async_copy(expand.at[0, way, mine], ini_s.at[way, pl.ds(0, 64)], isem.at[way]))
            loads.append(pltpu.make_async_copy(contract.at[0, way, mine], craw.at[way], isem.at[2 + way]))
        for copy in loads:
            copy.start()
        for copy in loads:
            copy.wait()
        every = rate[0]
        at_way = lax.broadcasted_iota(jnp.int32, every.shape, 0)
        at_head = lax.broadcasted_iota(jnp.int32, every.shape, 1)
        for way in range(2):
            ini_s[way, 64:128] = jnp.swapaxes(craw[way], 0, 1)
            picked = jnp.where((at_way == way) & (at_head == mine), every, 0.0)
            one = jnp.sum(picked, axis=(0, 1), keepdims=True) * (1.0 / (64 * MB))
            ini_s[way, 128:136] = jnp.broadcast_to(one, (8, 128))
            init_send(way).start()

    def push(ct, j):
        return send(
            stg.at[ct, j], xl.at[seg * chunks + ct], push_s.at[j, ct], ch_r.at[seg * chunks + ct],
            dev(heads * c + j + first, 2 * y + late, far),
        )

    lo = lax.broadcasted_iota(jnp.int32, (MB, 128), 1) < 64
    lo_half = lax.broadcasted_iota(jnp.int32, (MB // 2, 128), 1) < 64

    def project_role():
        load_in.wait()
        row = lax.broadcasted_iota(jnp.int32, (MB, 128), 0)
        io0 = lax.broadcasted_iota(jnp.int32, (128, 128), 0) // 64
        io1 = lax.broadcasted_iota(jnp.int32, (128, 128), 1) // 64
        ones = jnp.where(io0 == io1, 1.0 / 64, 0.0).astype(bf)

        def unit_rows(x):
            x = x.astype(bf).astype(f32)
            sq = x * x
            top = sq.astype(bf)
            low = (sq - top.astype(f32)).astype(bf)
            return x * lax.rsqrt(dot(top, ones) + dot(low, ones) + 1e-06)

        def one(t, _):
            ct = need_order(t)

            @pl.when(sec == 1)
            def _():
                hop(ct).wait_recv()
                for k in (1, 3, 2, 0):
                    direct(ct, k).start()

            for k in (1, 3, 2):
                arrived(2 * lax.rem(y + k, n_y) + c, ct)
                pass_on(ct, k).start()
            for k in (0, 1, 3, 2):
                arrived(2 * lax.rem(y + k, n_y) + 1 - c, ct)
            h = jnp.concatenate([hbuf[i, span(ct)] for i in range(n_head)], axis=1)
            proj = [dot(h, inw[i]) for i in range(3)]
            live = row + ct * MB < counts[0]
            for pair in range(heads // 2):
                at = slice(pair * 128, pair * 128 + 128)
                q = unit_rows(proj[0][:, at])
                k = unit_rows(proj[1][:, at])
                v = unit_rows(proj[2][:, at])
                d = jnp.where(live, k - v, 0.0)
                k = jnp.where(live, k, 0.0)
                top, bot = d[0 : MB // 2], d[MB // 2 :]
                stg[ct, 2 * pair, 0:64] = jnp.where(lo, q, pltpu.roll(k, 64, 1)).astype(bf)
                stg[ct, 2 * pair, 64:96] = jnp.where(lo_half, top, pltpu.roll(bot, 64, 1)).astype(bf)
                stg[ct, 2 * pair + 1, 0:64] = jnp.where(lo, pltpu.roll(q, 64, 1), k).astype(bf)
                stg[ct, 2 * pair + 1, 64:96] = jnp.where(lo_half, pltpu.roll(top, 64, 1), bot).astype(bf)
                push(ct, 2 * pair).start()
                push(ct, 2 * pair + 1).start()
            return 0

        lax.fori_loop(0, chunks, one, 0)

    def to_sibling(ct):
        return send(p1.at[ct], rs1.at[ct], rs1_s.at[ct], rs1_r.at[ct], dev(seg, sib, sec))

    def to_chip(ct, k):
        other = lax.rem(y + k, n_y)
        return send(p2.at[ct, k], rs2.at[ct, k], rs2_s.at[k, ct], rs2_r.at[k, ct], dev(seg, 2 * other + c, sec))

    def mix_in(ct, j):
        part = mixb.at[j, span(ct)]
        return send(part, part, mix_s.at[0], mix_r.at[j, ct], dev(seg, sib, sec))

    def columns(head):
        return pl.ds(pl.multiple_of(head * cols, 128), cols)

    def combine_role():
        load_out.wait()

        def multiply(ct):
            for j in range(heads):
                mix_in(ct, j).wait_recv()
            pairs = [mixb[2 * i, span(ct)] + mixb[2 * i + 1, span(ct)] for i in range(heads // 2)]
            mixture = jnp.concatenate(pairs, axis=1)
            for k in range(n_y):
                other = lax.rem(y + k, n_y)
                p1[ct, k] = dot(mixture, outw[:, columns(2 * other + 1 - c)]).astype(bf)
            to_sibling(ct).start()
            for k in range(n_y):
                other = lax.rem(y + k, n_y)
                p2f[ct, k] = dot(mixture, outw[:, columns(2 * other + c)])

        def reduce(ct):
            to_sibling(ct).wait_recv()
            for k in (1, 3, 2):
                p2[ct, k] = (p2f[ct, k] + rs1[ct, k].astype(f32)).astype(bf)
                to_chip(ct, k).start()

        def finish(t, _):
            ct = done_order(t)
            acc = p2f[ct, 0] + rs1[ct, 0].astype(f32)
            for k in (1, 3, 2):
                to_chip(ct, k).wait_recv()
                acc = acc + rs2[ct, k].astype(f32)
            panel[0, span(ct)] = (hbuf[hd, span(ct)].astype(f32) + acc).astype(bf)

            @pl.when(sec == 0)
            def _():
                hop(ct).start()

            return 0

        def two(t, _):
            @pl.when(t < chunks)
            def _():
                multiply(done_order(t))

            @pl.when(t > 0)
            def _():
                reduce(done_order(t - 1))

            return 0

        lax.fori_loop(0, chunks + 1, two, 0)
        lax.fori_loop(0, chunks, finish, 0)

    def at(i):
        return i + c * (nb - 1 - 2 * i)

    def landed(b):
        send(xl.at[b], xl.at[b], fw_s.at[0], ch_r.at[b], dev(seg, sib, sec)).wait_recv()

    def forward(i):
        b = at(i)
        return send(xl.at[b], xl.at[b], fw_s.at[i], ch_r.at[b], dev(seg, sib, sec))

    def exchange(i):
        return send(exs.at[i], exl.at[i], ex_s.at[i], ex_r.at[i], dev(seg, sib, sec))

    def give_back(i):
        b = at(i)
        return send(
            mxs.at[i - half], mixb.at[mine, span(lax.rem(b, chunks))], mix_s.at[i - half],
            mix_r.at[mine, lax.rem(b, chunks)], dev(b // chunks, 2 * y + cg, far),
        )

    def chain_role():
        init_send(0).wait_recv()
        u[...] = ini[0:64]
        w[...] = ini[64:128]
        sc = ini[128:129]
        ub[...] = jnp.zeros_like(ub)
        wk[...] = jnp.zeros_like(wk)
        ub[64:128] = ini[0:64].astype(bf)
        wk[64:128] = ini[64:128].astype(bf)
        landed(at(0))
        forward(0).start()
        z = dot(xl[at(0), 0:64], ub[0:128])

        def mixed(i, out):
            exchange(nb - 1 - i).wait_recv()
            both = jnp.where(lo, 0.0, out + exl[nb - 1 - i])
            both = jnp.where(lax.rem(mine, 2) == 0, pltpu.roll(both, 64, 1), both)
            mxs[i - half] = both.astype(bf)
            give_back(i).start()

        def early(i, carry):
            landed(at(i + 1))

            @pl.when(i + 1 < half)
            def _():
                forward(i + 1).start()

            before = jnp.maximum(i - 1, 0)
            zn, back, out = chain_step(xl, at(before), at(i), at(i + 1), carry[0], carry[1], sc, u, w, ub, wk)
            exs[before] = out

            @pl.when(i > 0)
            def _():
                exchange(before).start()

            return zn, back

        def later(i, carry):
            after = jnp.minimum(i + 1, nb - 1)

            @pl.when(i + 1 < nb)
            def _():
                landed(at(after))

            zn, back, out = chain_step(xl, at(i - 1), at(i), at(after), carry[0], carry[1], sc, u, w, ub, wk)
            mixed(i - 1, out)
            return zn, back

        carry = lax.fori_loop(0, half + 1, early, (z, jnp.zeros((64, 128), bf)))
        carry = lax.fori_loop(half + 1, nb, later, carry)
        last = xl[at(nb - 1), 0:64]
        ub[64:128] = (u[...] - dot_tn(last, carry[1])[64:128]).astype(bf)
        aq = smooth(dot(last, ub[64:192])).astype(bf)
        mixed(nb - 1, pltpu.roll(last.astype(f32), 64, 1) + dot_nt(aq, wk[...]))

        def drain(i, _):
            forward(i).wait_send()
            exchange(i).wait_send()
            give_back(half + i).wait_send()
            return 0

        lax.fori_loop(0, half, drain, 0)

    def turn(t, _):
        @pl.when(jnp.logical_and(in_chain, sec + t == 1))
        def _():
            chain_role()

        @pl.when(t == 0)
        def _():
            project_role()
            combine_role()

        return 0

    lax.fori_loop(0, 2, turn, 0)

    def drain(ct, _):
        for k in range(n_y):
            direct(ct, k).wait_send()
        for k in range(1, n_y):
            pass_on(ct, k).wait_send()
            to_chip(ct, k).wait_send()
        for j in range(heads):
            push(ct, j).wait_send()
        to_sibling(ct).wait_send()

        @pl.when(sec == 0)
        def _():
            hop(ct).wait_send()

        return 0

    lax.fori_loop(0, chunks, drain, 0)

    @pl.when(holder)
    def _():
        init_send(0).wait_send()
        init_send(1).wait_send()


def solution(mesh):
    n_seg, n_head = mesh.shape["seg"], mesh.shape["head"]
    placed = (
        P("seg", "head"),
        P("section", None, None, "head"),
        P("section", "head", None),
        P("section", None, "head", None, None),
        P("section", None, "head", None, None),
        P("section", None, "head"),
        P("seg"),
    )

    def local(tokens, in_weight, out_weight, expand_init, contract_init, inner_rate, seg_counts):
        rows, cols = tokens.shape
        heads = expand_init.shape[2]
        chunks = rows // MB
        nb = n_seg * chunks
        n_y = n_head // 2
        any_space = pl.BlockSpec(memory_space=pl.ANY)
        vmem = pl.BlockSpec(memory_space=pltpu.VMEM)
        smem = pl.BlockSpec(memory_space=pltpu.SMEM)
        dma = pltpu.SemaphoreType.DMA
        return pl.pallas_call(
            functools.partial(kernel, n_seg, n_head, heads),
            out_shape=jax.ShapeDtypeStruct((1, rows, cols), bf),
            in_specs=[any_space] * 5 + [vmem, smem],
            out_specs=vmem,
            scratch_shapes=[
                pltpu.VMEM(in_weight.shape[1:], bf),
                pltpu.VMEM(out_weight.shape[1:], bf),
                pltpu.VMEM((n_head, rows, cols), bf),
                pltpu.VMEM((chunks, heads, 96, 128), bf),
                pltpu.VMEM((nb, 96, 128), bf),
                pltpu.VMEM((2, 136, 128), f32),
                pltpu.VMEM((136, 128), f32),
                pltpu.VMEM((2, 128, 64), f32),
                pltpu.VMEM((nb // 2, 64, 128), f32),
                pltpu.VMEM((nb // 2, 64, 128), f32),
                pltpu.VMEM((nb // 2, 64, 128), bf),
                pltpu.VMEM((heads, rows, 128), bf),
                pltpu.VMEM((chunks, n_y, MB, cols), bf),
                pltpu.VMEM((chunks, n_y, MB, cols), f32),
                pltpu.VMEM((chunks, n_y, MB, cols), bf),
                pltpu.VMEM((chunks, n_y, MB, cols), bf),
                pltpu.VMEM((chunks, n_y, MB, cols), bf),
                pltpu.VMEM((64, 128), f32),
                pltpu.VMEM((64, 128), f32),
                pltpu.VMEM((192, 128), bf),
                pltpu.VMEM((128, 128), bf),
                dma((2,)),
                dma,
                dma((4,)),
                dma((2 * n_y - 1, chunks)),
                dma((n_head, chunks)),
                dma((chunks,)),
                dma((chunks,)),
                dma((heads, chunks)),
                dma((nb,)),
                dma((nb // 2,)),
                dma((nb // 2,)),
                dma((nb // 2,)),
                dma((nb // 2,)),
                dma((heads, chunks)),
                dma((chunks,)),
                dma((chunks,)),
                dma((n_y, chunks)),
                dma((n_y, chunks)),
                dma((2,)),
                dma,
            ],
            compiler_params=pltpu.CompilerParams(
                collective_id=0, has_side_effects=True, vmem_limit_bytes=44 << 20
            ),
            name="both_groups",
        )(tokens, in_weight, out_weight, expand_init, contract_init, inner_rate, seg_counts)

    return jax.shard_map(
        local, mesh=mesh, in_specs=placed, out_specs=P("section", "seg", "head"), check_vma=False
    )
```

time: 393 us -> 156 us (0.40)
  blocking collectives: 130 us -> 0 us
  waiting for transfers between devices: 129 us -> 0 us
  Pallas kernels: 62.2 us -> 149 us
  local copies, waits for them, and re-layouts: 22.8 us -> 6.17 us
  matrix products: 13.6 us -> 0 us
  between operations: 14.2 us -> 0.68 us
  other arithmetic: 10.9 us -> 0 us
  starting transfers between devices: 9.31 us -> 0 us
    pallas_call x2 -> x1, Pallas kernels: 62.2 us -> 149 us  [local(): pl.pallas_call(functools.partial(kernel, n_seg, n_head, heads), out_shape...]
    all_to_all x3 -> x0, blocking collectives: 83.9 us -> none  [the longest x1 45.9 us: layer(): got = lax.all_to_all(pieces, 'seg', 0, 0, tiled=True)]
    unnamed x6 -> x0, waiting for transfers between devices: 65.6 us -> none
    all_gather x2 -> x0, waiting for transfers between devices: 56.5 us -> none  [layer(): lax.all_gather(hidden, 'head', axis=1, tiled=True)]
    unnamed x1 -> x0, blocking collectives: 45.8 us -> none
    dot_general x4 -> x0, matrix products: 13.6 us -> none  [the longest x2 11 us: layer(): jnp.einsum('td,jdc->tjc', lax.all_gather(hidden, 'head', axis=1, tiled=Tr...]
    all_to_all x1 -> x0, starting transfers between devices: 7.9 us -> none  [layer(): got = lax.all_to_all(pieces, 'seg', 0, 0, tiled=True)]
    ppermute x1 -> x0, waiting for transfers between devices: 7.24 us -> none  [local(): lax.ppermute(earlier, 'section', [(i, i + 1) for i in range(n - 1)])]
  transfers between devices with their start and end apart: 6 -> 0, of which waited for: 5 -> 0; matrix products, arithmetic and copies ran while one was open for 1% -> 0% of each run, Pallas kernels for 0% -> 0%
where the time goes in v2:
time: 156 us
  Pallas kernels  149 us (96%)
  local copies, waits for them, and re-layouts  6.17 us (4%)
    pallas_call x1, Pallas kernels, local(): pl.pallas_call(functools.partial(kernel, n_seg, n_head, heads), out_shape...  149 us
    unnamed x10, local copies, waits for them, and re-layouts  6.17 us

profile of v2, /device:TPU:4, one launch (start us, length us, event | category | flops | bytes accessed | tf_op | source)
XLA Modules:
  0.0 156.1 jit_solution(17743428205196764404)
XLA Ops:
  0.7 1.3 copy.8.contract
  1.9 0.0 copy-start
  1.9 1.7 %copy-done = bf16[1,384,3072]{2,1,0:T(8,128)(2,1)S(1)} copy-done((bf16[1,384,3072]{2,1,0:T(8,128)(2,1)S(1)}, bf16[1,384,3072]{2,1,0:T(8,128)(2,1)}, u32[]{:S(2)}) %copy-start) | copy-done | bytes 2359320
  3.6 0.0 copy-start.1
  3.6 1.0 copy-done.1
  4.6 0.0 copy-start.2
  4.6 0.9 copy-done.2
  5.5 0.0 copy-start.3
  5.5 0.7 copy-done.3
  6.2 149.3 %both_groups.1 = bf16[1,192,384]{2,1,0:T(8,128)(2,1)S(1)} custom-call(bf16[192,384]{1,0:T(8,128)(2,1)S(1)} %copy-done.2, bf16[1,3,3072,384]{3,2,1,0:T(8,128)(2,1)} %in_w.1, bf16[1,384,3072]{2,1,0:T(8,128)(2,1)S(1)} %copy-done, f32[1,2,6,64,128]{4,3,2,1,0:T(8,128)S(1)} %copy-done.1, f32[1,2,6,128,64]{4,3,2,1,0:T(8,128)S(1)} %copy.8.contract, ...), custom_call_target="tpu_custom_call" | custom-call | tf_op jit(solution)/shard_map/both_groups/pallas_call | solution.py:474
  155.5 0.7 copy.11
Async XLA Ops:
  1.9 1.7 %copy-start = (bf16[1,384,3072]{2,1,0:T(8,128)(2,1)S(1)}, bf16[1,384,3072]{2,1,0:T(8,128)(2,1)}, u32[]{:S(2)}) copy-start(bf16[1,384,3072]{2,1,0:T(8,128)(2,1)} %out_w.1) | copy-start | bytes 7077892
  3.6 1.0 copy-start.1
  4.6 0.9 copy-start.2
  5.5 0.7 copy-start.3

commit v3 on v2

--- a/solution.py
+++ b/solution.py
@@ -48,23 +48,20 @@
     s = s * sc
     ab = a.astype(bf)
     wkv = wk[...]
-    p = dot_nt(ab, wkv)
+    delta = jnp.where(hi, jnp.concatenate([pltpu.roll(dp, 64, 1), dp], 0), 0.0)
+    e = delta + dot(ab, wkv)
+    back = (dot_nt(e.astype(bf), wkv) * s).astype(bf)
     un = u[...] - dot_tn(xp, bk)[64:128]
     u[...] = un
     ub[64:128] = un.astype(bf)
-    zu = dot(xn, ub[0:128])
     zq = dot(xp, ub[64:192])
-    delta = jnp.where(hi, jnp.concatenate([pltpu.roll(dp, 64, 1), dp], 0), 0.0)
-    e = delta + p
-    f = dot(e.astype(bf), wkv)
-    back = (f * s).astype(bf)
     gram = dot_nt(jnp.where(hi, xn, jnp.zeros_like(xn)), xb).astype(bf)
-    zn = zu - dot(gram, back)
+    zn = dot(xn, ub[0:128]) - dot(gram, back)
     aq = smooth(zq).astype(bf)
-    out = pltpu.roll(xp.astype(f32), 64, 1) + dot_nt(aq, wkv)
-    wn = w[...] - dot_tn((e * sc).astype(bf), ab)[64:128]
+    out = pltpu.roll(xp.astype(f32), 64, 1) + dot(aq, wkv)
+    wn = w[...] - dot_tn(ab, (e * sc).astype(bf))
     w[...] = wn
-    wk[64:128] = wn.astype(bf)
+    wk[...] = wn.astype(bf)
     return zn, back, out
 
 
@@ -72,9 +69,9 @@
     n_seg, n_head, heads,
     tokens, in_w, out_w, expand, contract, rate, counts,
     panel,
-    inw, outw, hbuf, stg, xl, ini_s, ini, craw, exs, exl, mxs, mixb,
+    inw, outw, hbuf, stg, xl, ini_s, ini, exs, exl, mxs, mixb,
     p1, p2f, rs1, p2, rs2, u, w, ub, wk,
-    wsem, tsem, isem, ag_s, ag_r, hop_s, hop_r, push_s, ch_r, fw_s, ex_s, ex_r,
+    wsem, tsem, isem, ag_s, ag_r, po_s, hop_s, push_s, ch_r, fw_s, fw_r, ex_s, ex_r,
     mix_s, mix_r, rs1_s, rs1_r, rs2_s, rs2_r, ini_ss, ini_r,
 ):
     rows = tokens.shape[0]
@@ -83,8 +80,8 @@
     nb = n_seg * chunks
     half = nb // 2
     n_y = n_head // 2
-    units = 2 * heads
-    first = (n_seg - units) // 2
+    line = n_seg // 2
+    turn_by = line // 2 + 1
     sec = lax.axis_index("section")
     seg = lax.axis_index("seg")
     hd = lax.axis_index("head")
@@ -92,11 +89,16 @@
     c = lax.rem(hd, 2)
     sib = 2 * y + 1 - c
     far = 1 - sec
-    late = seg // (n_seg // 2)
-    in_chain = jnp.logical_and(seg >= first, seg < first + units)
-    unit = seg - first
-    cg = unit // heads
-    mine = unit - cg * heads
+    late = seg // line
+    spot = lax.rem(lax.rem(seg, line) + line - turn_by, line)
+    in_chain = spot < heads
+    cg = late
+    mine = jnp.minimum(spot, heads - 1)
+    edge = jnp.logical_or(seg < 2, seg >= n_seg - 2)
+
+    def place(group, j):
+        return group * line + lax.rem(j + turn_by, line)
+
     holder = jnp.logical_and(in_chain, cg == c)
 
     def dev(s, h, x):
@@ -127,89 +129,99 @@
     def greet(device):
         pl.semaphore_signal(barrier, inc=1, device_id=device, device_id_type=pl.DeviceIdType.MESH)
 
+    for j in range(heads):
+        greet(dev(place(c, j), 2 * y + 1 - late, far))
+
+    @pl.when(in_chain)
+    def _():
+        for k in range(line):
+            greet(dev(c * line + k, 2 * y + cg, far))
+        greet(dev(seg, 2 * y + cg, far))
+
+    @pl.when(sec == 1)
+    def _():
+        for k in range(n_y):
+            greet(dev(seg, 2 * k + c, 0))
+
     for k in range(1, n_head):
         greet(dev(seg, lax.rem(hd + k, n_head), sec))
-
-    @pl.when(sec == 1)
-    def _():
-        greet(dev(seg, hd, 0))
-
-    for j in range(heads):
-        greet(dev(heads * c + j + first, 2 * y + 1 - late, far))
-
-    @pl.when(in_chain)
-    def _():
-        for k in range(n_seg // 2):
-            greet(dev(c * (n_seg // 2) + k, 2 * y + cg, far))
-        greet(dev(seg, 2 * y + cg, far))
-
-    total = n_head - 1 + heads + (1 - sec)
-    total = total + jnp.where(in_chain, n_seg // 2, 0) + jnp.where(holder, 2, 0)
-    pl.semaphore_wait(barrier, total)
-
-    def direct(ct, k):
-        to = jnp.int32(sib) if k == 0 else 2 * lax.rem(y + k, n_y) + c
-        part = hbuf.at[hd, span(ct)]
-        return send(part, part, ag_s.at[k, ct], ag_r.at[hd, ct], dev(seg, to, sec))
-
-    def pass_on(ct, k):
-        slot = 2 * lax.rem(y + k, n_y) + c
-        part = hbuf.at[slot, span(ct)]
-        return send(part, part, ag_s.at[n_y - 1 + k, ct], ag_r.at[slot, ct], dev(seg, sib, sec))
-
-    def hop(ct):
-        return send(panel.at[0, span(ct)], hbuf.at[hd, span(ct)], hop_s.at[ct], hop_r.at[ct], dev(seg, hd, 1))
-
-    def arrived(slot, ct):
-        part = hbuf.at[slot, span(ct)]
-        send(part, part, ag_s.at[0, ct], ag_r.at[slot, ct], dev(seg, sib, sec)).wait_recv()
-
-    flip = lax.rem(late + sec, 2)
-
-    def need_order(t):
-        return t + flip * (chunks - 1 - 2 * t)
-
-    def done_order(t):
-        return t + (1 - late) * (chunks - 1 - 2 * t)
-
-    @pl.when(sec == 0)
-    def _():
-        load_tok.wait()
-
-        def go(t, _):
-            for k in (1, 3, 2, 0):
-                direct(need_order(t), k).start()
-            return 0
-
-        lax.fori_loop(0, chunks, go, 0)
-
-    def init_send(way):
-        return send(ini_s.at[way], ini, ini_ss.at[way], ini_r, dev(seg, 2 * y + way, far))
 
     @pl.when(holder)
     def _():
         loads = []
         for way in range(2):
             loads.append(pltpu.make_async_copy(expand.at[0, way, mine], ini_s.at[way, pl.ds(0, 64)], isem.at[way]))
-            loads.append(pltpu.make_async_copy(contract.at[0, way, mine], craw.at[way], isem.at[2 + way]))
+            loads.append(
+                pltpu.make_async_copy(contract.at[0, way, mine], ini_s.at[way, pl.ds(64, 64)], isem.at[2 + way])
+            )
         for copy in loads:
             copy.start()
-        for copy in loads:
-            copy.wait()
         every = rate[0]
         at_way = lax.broadcasted_iota(jnp.int32, every.shape, 0)
         at_head = lax.broadcasted_iota(jnp.int32, every.shape, 1)
         for way in range(2):
-            ini_s[way, 64:128] = jnp.swapaxes(craw[way], 0, 1)
             picked = jnp.where((at_way == way) & (at_head == mine), every, 0.0)
             one = jnp.sum(picked, axis=(0, 1), keepdims=True) * (1.0 / (64 * MB))
             ini_s[way, 128:136] = jnp.broadcast_to(one, (8, 128))
-            init_send(way).start()
+        for copy in loads:
+            copy.wait()
+
+    @pl.when(sec == 0)
+    def _():
+        load_tok.wait()
+
+    total = n_head - 1 + heads + n_y * (1 - sec)
+    total = total + jnp.where(in_chain, line, 0) + jnp.where(holder, 2, 0)
+    pl.semaphore_wait(barrier, total)
+
+    def direct(ct, k):
+        part = hbuf.at[hd, span(ct)]
+        return send(part, part, ag_s.at[k, ct], ag_r.at[hd, ct], dev(seg, 2 * lax.rem(y + k, n_y) + c, sec))
+
+    def hop(ct, k):
+        return send(
+            panel.at[0, span(ct)], hbuf.at[hd, span(ct)], hop_s.at[k, ct], ag_r.at[hd, ct],
+            dev(seg, 2 * lax.rem(y + k, n_y) + c, 1),
+        )
+
+    def pass_on(ct, k):
+        slot = 2 * lax.rem(y + k, n_y) + c
+        part = hbuf.at[slot, span(ct)]
+        return send(part, part, po_s.at[k, ct], ag_r.at[slot, ct], dev(seg, sib, sec))
+
+    def arrived(slot, ct):
+        part = hbuf.at[slot, span(ct)]
+        send(part, part, po_s.at[0, ct], ag_r.at[slot, ct], dev(seg, sib, sec)).wait_recv()
+
+    flip = lax.rem(late + sec, 2)
+
+    def need_order(t):
+        return t + flip * (chunks - 1 - 2 * t)
+
+    def done_order(t):
+        return t + (1 - late) * (chunks - 1 - 2 * t)
+
+    @pl.when(sec == 0)
+    def _():
+        def go(t, _):
+            for k in (2, 1, 3):
+                direct(need_order(t), k).start()
+            return 0
+
+        lax.fori_loop(0, chunks, go, 0)
+
+    def init_send(way):
+        return send(ini_s.at[way], ini, ini_ss.at[way], ini_r, dev(seg, 2 * y + way, far))
+
+    @pl.when(holder)
+    def _():
+        init_send(0).start()
+        init_send(1).start()
 
     def push(ct, j):
         return send(
             stg.at[ct, j], xl.at[seg * chunks + ct], push_s.at[j, ct], ch_r.at[seg * chunks + ct],
-            dev(heads * c + j + first, 2 * y + late, far),
+            dev(place(c, j), 2 * y + late, far),
         )
 
     lo = lax.broadcasted_iota(jnp.int32, (MB, 128), 1) < 64
@@ -234,10 +246,9 @@
 
             @pl.when(sec == 1)
             def _():
-                hop(ct).wait_recv()
-                for k in (1, 3, 2, 0):
-                    direct(ct, k).start()
-
+                arrived(hd, ct)
+
+            pass_on(ct, 0).start()
             for k in (1, 3, 2):
                 arrived(2 * lax.rem(y + k, n_y) + c, ct)
                 pass_on(ct, k).start()
@@ -258,11 +269,24 @@
                 stg[ct, 2 * pair, 64:96] = jnp.where(lo_half, top, pltpu.roll(bot, 64, 1)).astype(bf)
                 stg[ct, 2 * pair + 1, 0:64] = jnp.where(lo, pltpu.roll(q, 64, 1), k).astype(bf)
                 stg[ct, 2 * pair + 1, 64:96] = jnp.where(lo_half, pltpu.roll(top, 64, 1), bot).astype(bf)
-                push(ct, 2 * pair).start()
-                push(ct, 2 * pair + 1).start()
+
+                @pl.when(edge)
+                def _():
+                    push(ct, 2 * pair).start()
+                    push(ct, 2 * pair + 1).start()
+
             return 0
 
         lax.fori_loop(0, chunks, one, 0)
+
+        @pl.when(jnp.logical_not(edge))
+        def _():
+            def rest(t, _):
+                for j in range(heads):
+                    push(need_order(t), j).start()
+                return 0
+
+            lax.fori_loop(0, chunks, rest, 0)
 
     def to_sibling(ct):
         return send(p1.at[ct], rs1.at[ct], rs1_s.at[ct], rs1_r.at[ct], dev(seg, sib, sec))
@@ -310,7 +334,8 @@
 
             @pl.when(sec == 0)
             def _():
-                hop(ct).start()
+                for k in (2, 1, 3, 0):
+                    hop(ct, k).start()
 
             return 0
 
@@ -331,15 +356,22 @@
     def at(i):
         return i + c * (nb - 1 - 2 * i)
 
-    def landed(b):
+    def landed(i):
+        b = at(i)
         send(xl.at[b], xl.at[b], fw_s.at[0], ch_r.at[b], dev(seg, sib, sec)).wait_recv()
 
-    def forward(i):
-        b = at(i)
-        return send(xl.at[b], xl.at[b], fw_s.at[i], ch_r.at[b], dev(seg, sib, sec))
-
-    def exchange(i):
-        return send(exs.at[i], exl.at[i], ex_s.at[i], ex_r.at[i], dev(seg, sib, sec))
+    def three(g):
+        return xl.at[pl.ds((g + c * (n_seg - 1 - 2 * g)) * chunks, chunks)]
+
+    def forward(g):
+        return send(three(g), three(g), fw_s.at[g], fw_r.at[g], dev(seg, sib, sec))
+
+    def other_half(g):
+        back = n_seg - 1 - g
+        send(three(g), three(g), fw_s.at[back], fw_r.at[back], dev(seg, sib, sec)).wait_recv()
+
+    def exchange(g):
+        return send(exs.at[g], exl.at[g], ex_s.at[g], ex_r.at[g], dev(seg, sib, sec))
 
     def give_back(i):
         b = at(i)
@@ -349,67 +381,97 @@
         )
 
     def chain_role():
+        ub[...] = jnp.zeros_like(ub)
         init_send(0).wait_recv()
         u[...] = ini[0:64]
-        w[...] = ini[64:128]
+        ub[64:128] = ini[0:64].astype(bf)
+        w0 = jnp.concatenate([jnp.zeros((128, 64), f32), jnp.swapaxes(ini[64:128], 0, 1)], axis=1)
+        w[...] = w0
+        wk[...] = w0.astype(bf)
         sc = ini[128:129]
-        ub[...] = jnp.zeros_like(ub)
-        wk[...] = jnp.zeros_like(wk)
-        ub[64:128] = ini[0:64].astype(bf)
-        wk[64:128] = ini[64:128].astype(bf)
-        landed(at(0))
-        forward(0).start()
+        landed(0)
         z = dot(xl[at(0), 0:64], ub[0:128])
 
-        def mixed(i, out):
-            exchange(nb - 1 - i).wait_recv()
-            both = jnp.where(lo, 0.0, out + exl[nb - 1 - i])
+        def mixed(m, t, mine_out):
+            i = chunks * m + t - 1
+            slot = nb + 1 - chunks * m - t
+            both = mine_out + exl[slot // chunks, lax.rem(slot, chunks)]
+            both = jnp.where(lo, 0.0, both)
             both = jnp.where(lax.rem(mine, 2) == 0, pltpu.roll(both, 64, 1), both)
             mxs[i - half] = both.astype(bf)
             give_back(i).start()
 
-        def early(i, carry):
-            landed(at(i + 1))
-
-            @pl.when(i + 1 < half)
-            def _():
-                forward(i + 1).start()
-
-            before = jnp.maximum(i - 1, 0)
-            zn, back, out = chain_step(xl, at(before), at(i), at(i + 1), carry[0], carry[1], sc, u, w, ub, wk)
-            exs[before] = out
-
-            @pl.when(i > 0)
-            def _():
-                exchange(before).start()
-
-            return zn, back
-
-        def later(i, carry):
-            after = jnp.minimum(i + 1, nb - 1)
-
-            @pl.when(i + 1 < nb)
-            def _():
-                landed(at(after))
-
-            zn, back, out = chain_step(xl, at(i - 1), at(i), at(after), carry[0], carry[1], sc, u, w, ub, wk)
-            mixed(i - 1, out)
-            return zn, back
-
-        carry = lax.fori_loop(0, half + 1, early, (z, jnp.zeros((64, 128), bf)))
-        carry = lax.fori_loop(half + 1, nb, later, carry)
+        def group(g, carry):
+            @pl.when(g == 0)
+            def _():
+                for i in range(1, chunks + 1):
+                    landed(i)
+                forward(0).start()
+
+            @pl.when(g == 1)
+            def _():
+                for i in range(chunks + 1, 2 * chunks):
+                    landed(i)
+                forward(1).start()
+
+            @pl.when(jnp.logical_and(g >= 1, g < line - 1))
+            def _():
+                for i in range(chunks):
+                    landed(chunks * (g + 1) + i)
+                forward(g + 1).start()
+
+            @pl.when(jnp.logical_and(g >= line - 1, g < n_seg - 1))
+            def _():
+                other_half(g + 1)
+
+            z, back = carry
+            for t in range(chunks):
+                i = chunks * g + t
+                before, after = jnp.maximum(i - 1, 0), jnp.minimum(i + 1, nb - 1)
+                z, back, out = chain_step(xl, at(before), at(i), at(after), z, back, sc, u, w, ub, wk)
+                exs[g, t] = out
+
+            @pl.when(g <= line)
+            def _():
+                exchange(g).start()
+
+            @pl.when(g > line)
+            def _():
+                m = g - 1
+
+                @pl.when(m == line)
+                def _():
+                    exchange(line).wait_recv()
+
+                exchange(n_seg - 1 - m).wait_recv()
+
+                @pl.when(m > line)
+                def _():
+                    mixed(m, 0, exs[m, 0])
+
+                for t in range(1, chunks):
+                    mixed(m, t, exs[m, t])
+
+            return z, back
+
+        carry = lax.fori_loop(0, n_seg, group, (z, jnp.zeros((64, 128), bf)))
+        exchange(0).wait_recv()
+        for t in range(chunks):
+            mixed(n_seg - 1, t, exs[n_seg - 1, t])
         last = xl[at(nb - 1), 0:64]
         ub[64:128] = (u[...] - dot_tn(last, carry[1])[64:128]).astype(bf)
         aq = smooth(dot(last, ub[64:192])).astype(bf)
-        mixed(nb - 1, pltpu.roll(last.astype(f32), 64, 1) + dot_nt(aq, wk[...]))
+        mixed(n_seg, 0, pltpu.roll(last.astype(f32), 64, 1) + dot(aq, wk[...]))
 
         def drain(i, _):
-            forward(i).wait_send()
-            exchange(i).wait_send()
             give_back(half + i).wait_send()
             return 0
 
         lax.fori_loop(0, half, drain, 0)
+        for g in range(line):
+            forward(g).wait_send()
+        for g in range(line + 1):
+            exchange(g).wait_send()
 
     def turn(t, _):
         @pl.when(jnp.logical_and(in_chain, sec + t == 1))
@@ -427,9 +489,8 @@
 
     def drain(ct, _):
         for k in range(n_y):
-            direct(ct, k).wait_send()
+            pass_on(ct, k).wait_send()
         for k in range(1, n_y):
-            pass_on(ct, k).wait_send()
             to_chip(ct, k).wait_send()
         for j in range(heads):
             push(ct, j).wait_send()
@@ -437,7 +498,10 @@
 
         @pl.when(sec == 0)
         def _():
-            hop(ct).wait_send()
+            for k in range(n_y):
+                hop(ct, k).wait_send()
+            for k in range(1, n_y):
+                direct(ct, k).wait_send()
 
         return 0
 
@@ -467,7 +531,7 @@
         chunks = rows // MB
         nb = n_seg * chunks
         n_y = n_head // 2
-        any_space = pl.BlockSpec(memory_space=pl.ANY)
+        any_space = pl.BlockSpec(memory_space=pltpu.HBM)
         vmem = pl.BlockSpec(memory_space=pltpu.VMEM)
         smem = pl.BlockSpec(memory_space=pltpu.SMEM)
         dma = pltpu.SemaphoreType.DMA
@@ -484,9 +548,8 @@
                 pltpu.VMEM((nb, 96, 128), bf),
                 pltpu.VMEM((2, 136, 128), f32),
                 pltpu.VMEM((136, 128), f32),
-                pltpu.VMEM((2, 128, 64), f32),
-                pltpu.VMEM((nb // 2, 64, 128), f32),
-                pltpu.VMEM((nb // 2, 64, 128), f32),
+                pltpu.VMEM((n_seg, chunks, 64, 128), f32),
+                pltpu.VMEM((n_seg // 2 + 1, chunks, 64, 128), f32),
                 pltpu.VMEM((nb // 2, 64, 128), bf),
                 pltpu.VMEM((heads, rows, 128), bf),
                 pltpu.VMEM((chunks, n_y, MB, cols), bf),
@@ -495,21 +558,22 @@
                 pltpu.VMEM((chunks, n_y, MB, cols), bf),
                 pltpu.VMEM((chunks, n_y, MB, cols), bf),
                 pltpu.VMEM((64, 128), f32),
-                pltpu.VMEM((64, 128), f32),
+                pltpu.VMEM((128, 128), f32),
                 pltpu.VMEM((192, 128), bf),
                 pltpu.VMEM((128, 128), bf),
                 dma((2,)),
                 dma,
                 dma((4,)),
-                dma((2 * n_y - 1, chunks)),
+                dma((n_y, chunks)),
                 dma((n_head, chunks)),
-                dma((chunks,)),
-                dma((chunks,)),
+                dma((n_y, chunks)),
+                dma((n_y, chunks)),
                 dma((heads, chunks)),
                 dma((nb,)),
-                dma((nb // 2,)),
-                dma((nb // 2,)),
-                dma((nb // 2,)),
+                dma((n_seg // 2,)),
+                dma((n_seg // 2,)),
+                dma((n_seg // 2 + 1,)),
+                dma((n_seg // 2 + 1,)),
                 dma((nb // 2,)),
                 dma((heads, chunks)),
                 dma((chunks,)),
@@ -520,10 +584,10 @@
                 dma,
             ],
             compiler_params=pltpu.CompilerParams(
-                collective_id=0, has_side_effects=True, vmem_limit_bytes=44 << 20
+                collective_id=0, has_side_effects=True, vmem_limit_bytes=60 << 20
             ),
             name="both_groups",
-        )(tokens, in_weight, out_weight, expand_init, contract_init, inner_rate, seg_counts)
+        )(tokens, in_weight, out_weight, expand_init, jnp.swapaxes(contract_init, 3, 4), inner_rate, seg_counts)
 
     return jax.shard_map(
         local, mesh=mesh, in_specs=placed, out_specs=P("section", "seg", "head"), check_vma=False

time: 156 us -> 147 us (0.942)
  Pallas kernels: 149 us -> 144 us
  local copies, waits for them, and re-layouts: 6.17 us -> 1.59 us
    pallas_call x1, Pallas kernels: 149 us -> 144 us  [local(): pl.pallas_call(functools.partial(kernel, n_seg, n_head, heads), out_shape...]
    unnamed x10 -> x1, local copies, waits for them, and re-layouts: 6.17 us -> 1.59 us
where the time goes in v3:
time: 147 us
  Pallas kernels  144 us (98%)
  local copies, waits for them, and re-layouts  1.59 us (1%)
    pallas_call x1, Pallas kernels, local(): pl.pallas_call(functools.partial(kernel, n_seg, n_head, heads), out_shape...  144 us

profile of v3, /device:TPU:4, one launch (start us, length us, event | category | flops | bytes accessed | tf_op | source)
XLA Modules:
  0.0 146.5 jit_solution(1426123232211212257)
XLA Ops:
  0.7 144.3 %both_groups.1 = bf16[1,192,384]{2,1,0:T(8,128)(2,1)} custom-call(bf16[192,384]{1,0:T(8,128)(2,1)} %tokens.1, bf16[1,3,3072,384]{3,2,1,0:T(8,128)(2,1)} %in_w.1, bf16[1,384,3072]{2,1,0:T(8,128)(2,1)} %out_w.1, f32[1,2,6,64,128]{4,3,2,1,0:T(8,128)} %expand.1, f32[1,2,6,64,128]{4,3,2,1,0:T(8,128)} %bitcast.1, f32[1,2,6]{2,1,0:T(2,128)} %rate.1, s32[1]{0:T(128)S(6)} %copy.9.counts), custom_call_target="tpu_custom_call" | custom-call | tf_op jit(solution)/shard_map/both_groups/pallas_call | solution.py:538
  144.9 1.6 %copy.10 = bf16[1,192,384]{2,1,0:T(8,128)(2,1)} copy(bf16[1,192,384]{2,1,0:T(8,128)(2,1)} %both_groups.1) | data formatting | bytes 294912

commit v4 on v3

--- a/solution.py
+++ b/solution.py
@@ -69,9 +69,9 @@
     n_seg, n_head, heads,
     tokens, in_w, out_w, expand, contract, rate, counts,
     panel,
-    inw, outw, hbuf, stg, xl, ini_s, ini, exs, exl, mxs, mixb,
+    inw, outw, hbuf, acc, stg, xl, ini_s, ini, exs, exl, mxs, mixb,
     p1, p2f, rs1, p2, rs2, u, w, ub, wk,
-    wsem, tsem, isem, ag_s, ag_r, po_s, hop_s, push_s, ch_r, fw_s, fw_r, ex_s, ex_r,
+    wsem, tsem, isem, ag_s, ag_r, po_s, hop_s, push_s, ch_r, fw_s, ex_s, ex_r,
     mix_s, mix_r, rs1_s, rs1_r, rs2_s, rs2_r, ini_ss, ini_r,
 ):
     rows = tokens.shape[0]
@@ -88,13 +88,11 @@
     y = hd // 2
     c = lax.rem(hd, 2)
     sib = 2 * y + 1 - c
-    far = 1 - sec
     late = seg // line
     spot = lax.rem(lax.rem(seg, line) + line - turn_by, line)
     in_chain = spot < heads
     cg = late
     mine = jnp.minimum(spot, heads - 1)
-    edge = jnp.logical_or(seg < 2, seg >= n_seg - 2)
 
     def place(group, j):
         return group * line + lax.rem(j + turn_by, line)
@@ -130,18 +128,20 @@
         pl.semaphore_signal(barrier, inc=1, device_id=device, device_id_type=pl.DeviceIdType.MESH)
 
     for j in range(heads):
-        greet(dev(place(c, j), 2 * y + 1 - late, far))
+        greet(dev(place(c, j), 2 * y + 1 - late, sec))
 
     @pl.when(in_chain)
     def _():
         for k in range(line):
-            greet(dev(c * line + k, 2 * y + cg, far))
-        greet(dev(seg, 2 * y + cg, far))
+            source = c * line + k
+
+            @pl.when(jnp.logical_not(jnp.logical_and(holder, source == seg)))
+            def _():
+                greet(dev(source, 2 * y + cg, sec))
 
     @pl.when(sec == 1)
     def _():
-        for k in range(n_y):
-            greet(dev(seg, 2 * k + c, 0))
+        greet(dev(seg, hd, 0))
 
     for k in range(1, n_head):
         greet(dev(seg, lax.rem(hd + k, n_head), sec))
@@ -149,20 +149,18 @@
     @pl.when(holder)
     def _():
         loads = []
-        for way in range(2):
-            loads.append(pltpu.make_async_copy(expand.at[0, way, mine], ini_s.at[way, pl.ds(0, 64)], isem.at[way]))
-            loads.append(
-                pltpu.make_async_copy(contract.at[0, way, mine], ini_s.at[way, pl.ds(64, 64)], isem.at[2 + way])
-            )
+        for way, to in ((c, ini), (1 - c, ini_s)):
+            loads.append(pltpu.make_async_copy(expand.at[0, way, mine], to.at[pl.ds(0, 64)], isem.at[len(loads)]))
+            loads.append(pltpu.make_async_copy(contract.at[0, way, mine], to.at[pl.ds(64, 64)], isem.at[len(loads)]))
         for copy in loads:
             copy.start()
         every = rate[0]
         at_way = lax.broadcasted_iota(jnp.int32, every.shape, 0)
         at_head = lax.broadcasted_iota(jnp.int32, every.shape, 1)
-        for way in range(2):
+        for way, to in ((c, ini), (1 - c, ini_s)):
             picked = jnp.where((at_way == way) & (at_head == mine), every, 0.0)
             one = jnp.sum(picked, axis=(0, 1), keepdims=True) * (1.0 / (64 * MB))
-            ini_s[way, 128:136] = jnp.broadcast_to(one, (8, 128))
+            to[128:136] = jnp.broadcast_to(one, (8, 128))
         for copy in loads:
             copy.wait()
 
@@ -170,19 +168,16 @@
     def _():
         load_tok.wait()
 
-    total = n_head - 1 + heads + n_y * (1 - sec)
-    total = total + jnp.where(in_chain, line, 0) + jnp.where(holder, 2, 0)
+    total = n_head - 1 + heads + (1 - sec)
+    total = total + jnp.where(in_chain, line, 0) - jnp.where(holder, 1, 0)
     pl.semaphore_wait(barrier, total)
 
     def direct(ct, k):
         part = hbuf.at[hd, span(ct)]
         return send(part, part, ag_s.at[k, ct], ag_r.at[hd, ct], dev(seg, 2 * lax.rem(y + k, n_y) + c, sec))
 
-    def hop(ct, k):
-        return send(
-            panel.at[0, span(ct)], hbuf.at[hd, span(ct)], hop_s.at[k, ct], ag_r.at[hd, ct],
-            dev(seg, 2 * lax.rem(y + k, n_y) + c, 1),
-        )
+    def hop(ct):
+        return send(panel.at[0, span(ct)], hbuf.at[hd, span(ct)], hop_s.at[ct], ag_r.at[hd, ct], dev(seg, hd, 1))
 
     def pass_on(ct, k):
         slot = 2 * lax.rem(y + k, n_y) + c
@@ -210,29 +205,77 @@
 
         lax.fori_loop(0, chunks, go, 0)
 
-    def init_send(way):
-        return send(ini_s.at[way], ini, ini_ss.at[way], ini_r, dev(seg, 2 * y + way, far))
+    init_send = send(ini_s, ini, ini_ss, ini_r, dev(seg, sib, sec))
 
     @pl.when(holder)
     def _():
-        init_send(0).start()
-        init_send(1).start()
-
-    def push(ct, j):
+        init_send.start()
+
+    def push(j):
         return send(
-            stg.at[ct, j], xl.at[seg * chunks + ct], push_s.at[j, ct], ch_r.at[seg * chunks + ct],
-            dev(place(c, j), 2 * y + late, far),
+            stg.at[j], xl.at[pl.ds(seg * chunks, chunks)], push_s.at[j], ch_r.at[seg],
+            dev(place(c, j), 2 * y + late, sec),
         )
 
+    def give(j):
+        own = jnp.logical_and(holder, mine == j)
+
+        @pl.when(own)
+        def _():
+            pltpu.make_async_copy(stg.at[j], xl.at[pl.ds(seg * chunks, chunks)], ch_r.at[seg]).start()
+
+        @pl.when(jnp.logical_not(own))
+        def _():
+            push(j).start()
+
     lo = lax.broadcasted_iota(jnp.int32, (MB, 128), 1) < 64
-    lo_half = lax.broadcasted_iota(jnp.int32, (MB // 2, 128), 1) < 64
 
     def project_role():
+        def spread(t, _):
+            ct = need_order(t)
+
+            @pl.when(sec == 1)
+            def _():
+                arrived(hd, ct)
+                for k in (2, 1, 3):
+                    direct(ct, k).start()
+
+            pass_on(ct, 0).start()
+            return 0
+
+        def relay(t, _):
+            ct = need_order(t)
+            for k in (1, 3, 2):
+                arrived(2 * lax.rem(y + k, n_y) + c, ct)
+                pass_on(ct, k).start()
+            return 0
+
+        def add(k):
+            chip = lax.rem(y + k, n_y)
+
+            def await_one(t, _):
+                arrived(2 * chip + 1 - c, need_order(t))
+                return 0
+
+            lax.fori_loop(0, chunks, await_one, 0)
+            h = jnp.concatenate([hbuf[2 * chip], hbuf[2 * chip + 1]], axis=1)
+            at = pl.ds(pl.multiple_of(chip * 2 * cols, 128), 2 * cols)
+            for i in range(3):
+                part = dot(h, inw[i, at])
+                acc[i] = part if k == 0 else acc[i] + part
+
+        lax.fori_loop(0, chunks, spread, 0)
         load_in.wait()
-        row = lax.broadcasted_iota(jnp.int32, (MB, 128), 0)
+        add(0)
+        lax.fori_loop(0, chunks, relay, 0)
+        for k in (1, 3, 2):
+            add(k)
+
         io0 = lax.broadcasted_iota(jnp.int32, (128, 128), 0) // 64
         io1 = lax.broadcasted_iota(jnp.int32, (128, 128), 1) // 64
         ones = jnp.where(io0 == io1, 1.0 / 64, 0.0).astype(bf)
+        live = lax.broadcasted_iota(jnp.int32, (rows, 128), 0) < counts[0]
+        lo_all = lax.broadcasted_iota(jnp.int32, (rows, 128), 1) < 64
 
         def unit_rows(x):
             x = x.astype(bf).astype(f32)
@@ -241,52 +284,27 @@
             low = (sq - top.astype(f32)).astype(bf)
             return x * lax.rsqrt(dot(top, ones) + dot(low, ones) + 1e-06)
 
-        def one(t, _):
-            ct = need_order(t)
-
-            @pl.when(sec == 1)
-            def _():
-                arrived(hd, ct)
-
-            pass_on(ct, 0).start()
-            for k in (1, 3, 2):
-                arrived(2 * lax.rem(y + k, n_y) + c, ct)
-                pass_on(ct, k).start()
-            for k in (0, 1, 3, 2):
-                arrived(2 * lax.rem(y + k, n_y) + 1 - c, ct)
-            h = jnp.concatenate([hbuf[i, span(ct)] for i in range(n_head)], axis=1)
-            proj = [dot(h, inw[i]) for i in range(3)]
-            live = row + ct * MB < counts[0]
-            for pair in range(heads // 2):
-                at = slice(pair * 128, pair * 128 + 128)
-                q = unit_rows(proj[0][:, at])
-                k = unit_rows(proj[1][:, at])
-                v = unit_rows(proj[2][:, at])
-                d = jnp.where(live, k - v, 0.0)
-                k = jnp.where(live, k, 0.0)
-                top, bot = d[0 : MB // 2], d[MB // 2 :]
-                stg[ct, 2 * pair, 0:64] = jnp.where(lo, q, pltpu.roll(k, 64, 1)).astype(bf)
-                stg[ct, 2 * pair, 64:96] = jnp.where(lo_half, top, pltpu.roll(bot, 64, 1)).astype(bf)
-                stg[ct, 2 * pair + 1, 0:64] = jnp.where(lo, pltpu.roll(q, 64, 1), k).astype(bf)
-                stg[ct, 2 * pair + 1, 64:96] = jnp.where(lo_half, pltpu.roll(top, 64, 1), bot).astype(bf)
-
-                @pl.when(edge)
-                def _():
-                    push(ct, 2 * pair).start()
-                    push(ct, 2 * pair + 1).start()
-
-            return 0
-
-        lax.fori_loop(0, chunks, one, 0)
-
-        @pl.when(jnp.logical_not(edge))
-        def _():
-            def rest(t, _):
-                for j in range(heads):
-                    push(need_order(t), j).start()
-                return 0
-
-            lax.fori_loop(0, chunks, rest, 0)
+        for pair in range(heads // 2):
+            at = slice(pair * 128, pair * 128 + 128)
+            q = unit_rows(acc[0, :, at])
+            k = unit_rows(acc[1, :, at])
+            v = unit_rows(acc[2, :, at])
+            d = jnp.where(live, k - v, 0.0)
+            k = jnp.where(live, k, 0.0)
+            rolled = pltpu.roll(d, 64, 1)
+            even = jnp.where(lo_all, q, pltpu.roll(k, 64, 1)).astype(bf)
+            odd = jnp.where(lo_all, pltpu.roll(q, 64, 1), k).astype(bf)
+            for ct in range(chunks):
+                top = slice(ct * MB, ct * MB + MB // 2)
+                bot = slice(ct * MB + MB // 2, ct * MB + MB)
+                half_lo = lo[0 : MB // 2]
+                stg[2 * pair, ct, 0:64] = even[ct * MB : ct * MB + MB]
+                stg[2 * pair, ct, 64:96] = jnp.where(half_lo, d[top], rolled[bot]).astype(bf)
+                stg[2 * pair + 1, ct, 0:64] = odd[ct * MB : ct * MB + MB]
+                stg[2 * pair + 1, ct, 64:96] = jnp.where(half_lo, rolled[top], d[bot]).astype(bf)
+
+            give(2 * pair)
+            give(2 * pair + 1)
 
     def to_sibling(ct):
         return send(p1.at[ct], rs1.at[ct], rs1_s.at[ct], rs1_r.at[ct], dev(seg, sib, sec))
@@ -334,8 +352,7 @@
 
             @pl.when(sec == 0)
             def _():
-                for k in (2, 1, 3, 0):
-                    hop(ct, k).start()
+                hop(ct).start()
 
             return 0
 
@@ -356,19 +373,17 @@
     def at(i):
         return i + c * (nb - 1 - 2 * i)
 
-    def landed(i):
-        b = at(i)
-        send(xl.at[b], xl.at[b], fw_s.at[0], ch_r.at[b], dev(seg, sib, sec)).wait_recv()
+    def number(g):
+        return g + c * (n_seg - 1 - 2 * g)
 
     def three(g):
-        return xl.at[pl.ds((g + c * (n_seg - 1 - 2 * g)) * chunks, chunks)]
+        return xl.at[pl.ds(number(g) * chunks, chunks)]
 
     def forward(g):
-        return send(three(g), three(g), fw_s.at[g], fw_r.at[g], dev(seg, sib, sec))
-
-    def other_half(g):
-        back = n_seg - 1 - g
-        send(three(g), three(g), fw_s.at[back], fw_r.at[back], dev(seg, sib, sec)).wait_recv()
+        return send(three(g), three(g), fw_s.at[g], ch_r.at[number(g)], dev(seg, sib, sec))
+
+    def landed(g):
+        send(three(g), three(g), fw_s.at[0], ch_r.at[number(g)], dev(seg, sib, sec)).wait_recv()
 
     def exchange(g):
         return send(exs.at[g], exl.at[g], ex_s.at[g], ex_r.at[g], dev(seg, sib, sec))
@@ -377,12 +392,16 @@
         b = at(i)
         return send(
             mxs.at[i - half], mixb.at[mine, span(lax.rem(b, chunks))], mix_s.at[i - half],
-            mix_r.at[mine, lax.rem(b, chunks)], dev(b // chunks, 2 * y + cg, far),
+            mix_r.at[mine, lax.rem(b, chunks)], dev(b // chunks, 2 * y + cg, sec),
         )
 
     def chain_role():
         ub[...] = jnp.zeros_like(ub)
-        init_send(0).wait_recv()
+
+        @pl.when(jnp.logical_not(holder))
+        def _():
+            init_send.wait_recv()
+
         u[...] = ini[0:64]
         ub[64:128] = ini[0:64].astype(bf)
         w0 = jnp.concatenate([jnp.zeros((128, 64), f32), jnp.swapaxes(ini[64:128], 0, 1)], axis=1)
@@ -390,6 +409,8 @@
         wk[...] = w0.astype(bf)
         sc = ini[128:129]
         landed(0)
+        forward(0).start()
+
         z = dot(xl[at(0), 0:64], ub[0:128])
 
         def mixed(m, t, mine_out):
@@ -402,27 +423,13 @@
             give_back(i).start()
 
         def group(g, carry):
-            @pl.when(g == 0)
-            def _():
-                for i in range(1, chunks + 1):
-                    landed(i)
-                forward(0).start()
-
-            @pl.when(g == 1)
-            def _():
-                for i in range(chunks + 1, 2 * chunks):
-                    landed(i)
-                forward(1).start()
-
-            @pl.when(jnp.logical_and(g >= 1, g < line - 1))
-            def _():
-                for i in range(chunks):
-                    landed(chunks * (g + 1) + i)
+            @pl.when(g < n_seg - 1)
+            def _():
+                landed(g + 1)
+
+            @pl.when(g < line - 1)
+            def _():
                 forward(g + 1).start()
-
-            @pl.when(jnp.logical_and(g >= line - 1, g < n_seg - 1))
-            def _():
-                other_half(g + 1)
 
             z, back = carry
             for t in range(chunks):
@@ -473,44 +480,38 @@
         for g in range(line + 1):
             exchange(g).wait_send()
 
-    def turn(t, _):
-        @pl.when(jnp.logical_and(in_chain, sec + t == 1))
-        def _():
-            chain_role()
-
-        @pl.when(t == 0)
-        def _():
-            project_role()
-            combine_role()
-
-        return 0
-
-    lax.fori_loop(0, 2, turn, 0)
+    project_role()
+
+    @pl.when(in_chain)
+    def _():
+        chain_role()
+
+    combine_role()
 
     def drain(ct, _):
         for k in range(n_y):
             pass_on(ct, k).wait_send()
         for k in range(1, n_y):
+            direct(ct, k).wait_send()
             to_chip(ct, k).wait_send()
-        for j in range(heads):
-            push(ct, j).wait_send()
         to_sibling(ct).wait_send()
 
         @pl.when(sec == 0)
         def _():
-            for k in range(n_y):
-                hop(ct, k).wait_send()
-            for k in range(1, n_y):
-                direct(ct, k).wait_send()
+            hop(ct).wait_send()
 
         return 0
 
     lax.fori_loop(0, chunks, drain, 0)
+    for j in range(heads):
+
+        @pl.when(jnp.logical_not(jnp.logical_and(holder, mine == j)))
+        def _():
+            push(j).wait_send()
 
     @pl.when(holder)
     def _():
-        init_send(0).wait_send()
-        init_send(1).wait_send()
+        init_send.wait_send()
 
 
 def solution(mesh):
@@ -544,9 +545,10 @@
                 pltpu.VMEM(in_weight.shape[1:], bf),
                 pltpu.VMEM(out_weight.shape[1:], bf),
                 pltpu.VMEM((n_head, rows, cols), bf),
-                pltpu.VMEM((chunks, heads, 96, 128), bf),
+                pltpu.VMEM((3, rows, cols), f32),
+                pltpu.VMEM((heads, chunks, 96, 128), bf),
                 pltpu.VMEM((nb, 96, 128), bf),
-                pltpu.VMEM((2, 136, 128), f32),
+                pltpu.VMEM((136, 128), f32),
                 pltpu.VMEM((136, 128), f32),
                 pltpu.VMEM((n_seg, chunks, 64, 128), f32),
                 pltpu.VMEM((n_seg // 2 + 1, chunks, 64, 128), f32),
@@ -567,10 +569,9 @@
                 dma((n_y, chunks)),
                 dma((n_head, chunks)),
                 dma((n_y, chunks)),
-                dma((n_y, chunks)),
-                dma((heads, chunks)),
-                dma((nb,)),
-                dma((n_seg // 2,)),
+                dma((chunks,)),
+                dma((heads,)),
+                dma((n_seg,)),
                 dma((n_seg // 2,)),
                 dma((n_seg // 2 + 1,)),
                 dma((n_seg // 2 + 1,)),
@@ -580,7 +581,7 @@
                 dma((chunks,)),
                 dma((n_y, chunks)),
                 dma((n_y, chunks)),
-                dma((2,)),
+                dma,
                 dma,
             ],
             compiler_params=pltpu.CompilerParams(

time: 147 us -> 143 us (0.973)
  Pallas kernels: 144 us -> 140 us
    pallas_call x1, Pallas kernels: 144 us -> 140 us  [local(): pl.pallas_call(functools.partial(kernel, n_seg, n_head, heads), out_shape...]
where the time goes in v4:
time: 143 us
  Pallas kernels  140 us (98%)
  local copies, waits for them, and re-layouts  1.59 us (1%)
    pallas_call x1, Pallas kernels, local(): pl.pallas_call(functools.partial(kernel, n_seg, n_head, heads), out_shape...  140 us

profile of v4, /device:TPU:4, one launch (start us, length us, event | category | flops | bytes accessed | tf_op | source)
XLA Modules:
  0.0 142.7 jit_solution(10371478162978327987)
XLA Ops:
  0.7 140.5 %both_groups.1 = bf16[1,192,384]{2,1,0:T(8,128)(2,1)} custom-call(bf16[192,384]{1,0:T(8,128)(2,1)} %tokens.1, bf16[1,3,3072,384]{3,2,1,0:T(8,128)(2,1)} %in_w.1, bf16[1,384,3072]{2,1,0:T(8,128)(2,1)} %out_w.1, f32[1,2,6,64,128]{4,3,2,1,0:T(8,128)} %expand.1, f32[1,2,6,64,128]{4,3,2,1,0:T(8,128)} %bitcast.1, f32[1,2,6]{2,1,0:T(2,128)} %rate.1, s32[1]{0:T(128)S(6)} %copy.9.counts), custom_call_target="tpu_custom_call" | custom-call | tf_op jit(solution)/shard_map/both_groups/pallas_call | solution.py:539
  141.2 1.6 %copy.10 = bf16[1,192,384]{2,1,0:T(8,128)(2,1)} copy(bf16[1,192,384]{2,1,0:T(8,128)(2,1)} %both_groups.1) | data formatting | bytes 294912

commit v5 on v4

--- a/solution.py
+++ b/solution.py
@@ -71,7 +71,7 @@
     panel,
     inw, outw, hbuf, acc, stg, xl, ini_s, ini, exs, exl, mxs, mixb,
     p1, p2f, rs1, p2, rs2, u, w, ub, wk,
-    wsem, tsem, isem, ag_s, ag_r, po_s, hop_s, push_s, ch_r, fw_s, ex_s, ex_r,
+    wsem, tsem, isem, ag_s, ag_r, po_s, hop_s, push_s, ch_r, fw_s, fw_r, ex_s, ex_r,
     mix_s, mix_r, rs1_s, rs1_r, rs2_s, rs2_r, ini_ss, ini_r,
 ):
     rows = tokens.shape[0]
@@ -211,26 +211,45 @@
     def _():
         init_send.start()
 
-    def push(j):
+    part_first = (flip * (chunks - 1), 1 - flip)
+    part_size = (1, chunks - 1)
+
+    def block(p):
+        return pl.ds(seg * chunks + part_first[p], part_size[p])
+
+    def push(j, p):
         return send(
-            stg.at[j], xl.at[pl.ds(seg * chunks, chunks)], push_s.at[j], ch_r.at[seg],
+            stg.at[j, pl.ds(part_first[p], part_size[p])], xl.at[block(p)], push_s.at[j, p], ch_r.at[seg, p],
             dev(place(c, j), 2 * y + late, sec),
         )
 
-    def give(j):
+    def give(j, p):
         own = jnp.logical_and(holder, mine == j)
 
         @pl.when(own)
         def _():
-            pltpu.make_async_copy(stg.at[j], xl.at[pl.ds(seg * chunks, chunks)], ch_r.at[seg]).start()
+            pltpu.make_async_copy(
+                stg.at[j, pl.ds(part_first[p], part_size[p])], xl.at[block(p)], ch_r.at[seg, p]
+            ).start()
 
         @pl.when(jnp.logical_not(own))
         def _():
-            push(j).start()
+            push(j, p).start()
 
     lo = lax.broadcasted_iota(jnp.int32, (MB, 128), 1) < 64
 
     def project_role():
+        io0 = lax.broadcasted_iota(jnp.int32, (128, 128), 0) // 64
+        io1 = lax.broadcasted_iota(jnp.int32, (128, 128), 1) // 64
+        ones = jnp.where(io0 == io1, 1.0 / 64, 0.0).astype(bf)
+
+        def unit_rows(x):
+            x = x.astype(bf).astype(f32)
+            sq = x * x
+            top = sq.astype(bf)
+            low = (sq - top.astype(f32)).astype(bf)
+            return x * lax.rsqrt(dot(top, ones) + dot(low, ones) + 1e-06)
+
         def spread(t, _):
             ct = need_order(t)
 
@@ -250,61 +269,63 @@
                 pass_on(ct, k).start()
             return 0
 
-        def add(k):
-            chip = lax.rem(y + k, n_y)
-
-            def await_one(t, _):
-                arrived(2 * chip + 1 - c, need_order(t))
-                return 0
-
-            lax.fori_loop(0, chunks, await_one, 0)
-            h = jnp.concatenate([hbuf[2 * chip], hbuf[2 * chip + 1]], axis=1)
-            at = pl.ds(pl.multiple_of(chip * 2 * cols, 128), 2 * cols)
-            for i in range(3):
-                part = dot(h, inw[i, at])
-                acc[i] = part if k == 0 else acc[i] + part
-
-        lax.fori_loop(0, chunks, spread, 0)
-        load_in.wait()
-        add(0)
-        lax.fori_loop(0, chunks, relay, 0)
-        for k in (1, 3, 2):
-            add(k)
-
-        io0 = lax.broadcasted_iota(jnp.int32, (128, 128), 0) // 64
-        io1 = lax.broadcasted_iota(jnp.int32, (128, 128), 1) // 64
-        ones = jnp.where(io0 == io1, 1.0 / 64, 0.0).astype(bf)
-        live = lax.broadcasted_iota(jnp.int32, (rows, 128), 0) < counts[0]
-        lo_all = lax.broadcasted_iota(jnp.int32, (rows, 128), 1) < 64
-
-        def unit_rows(x):
-            x = x.astype(bf).astype(f32)
-            sq = x * x
-            top = sq.astype(bf)
-            low = (sq - top.astype(f32)).astype(bf)
-            return x * lax.rsqrt(dot(top, ones) + dot(low, ones) + 1e-06)
-
-        for pair in range(heads // 2):
-            at = slice(pair * 128, pair * 128 + 128)
-            q = unit_rows(acc[0, :, at])
-            k = unit_rows(acc[1, :, at])
-            v = unit_rows(acc[2, :, at])
-            d = jnp.where(live, k - v, 0.0)
-            k = jnp.where(live, k, 0.0)
-            rolled = pltpu.roll(d, 64, 1)
-            even = jnp.where(lo_all, q, pltpu.roll(k, 64, 1)).astype(bf)
-            odd = jnp.where(lo_all, pltpu.roll(q, 64, 1), k).astype(bf)
-            for ct in range(chunks):
-                top = slice(ct * MB, ct * MB + MB // 2)
-                bot = slice(ct * MB + MB // 2, ct * MB + MB)
+        def part(p):
+            times = (0, 1) if p == 0 else (1, chunks)
+            size = part_size[p] * MB
+            begin = pl.multiple_of(part_first[p] * MB, MB)
+            span_p = pl.ds(begin, size)
+
+            def add(k):
+                chip = lax.rem(y + k, n_y)
+
+                def await_one(t, _):
+                    arrived(2 * chip + 1 - c, need_order(t))
+                    return 0
+
+                lax.fori_loop(*times, await_one, 0)
+                h = jnp.concatenate([hbuf[2 * chip, span_p], hbuf[2 * chip + 1, span_p]], axis=1)
+                at = pl.ds(pl.multiple_of(chip * 2 * cols, 128), 2 * cols)
+                for i in range(3):
+                    term = dot(h, inw[i, at])
+                    acc[i, 0:size] = term if k == 0 else acc[i, 0:size] + term
+
+            if p == 0:
+                lax.fori_loop(*times, spread, 0)
+                load_in.wait()
+                add(0)
+                lax.fori_loop(*times, relay, 0)
+                lax.fori_loop(1, chunks, spread, 0)
+            else:
+                add(0)
+                lax.fori_loop(*times, relay, 0)
+            for k in (1, 3, 2):
+                add(k)
+            live = lax.broadcasted_iota(jnp.int32, (size, 128), 0) + begin < counts[0]
+            lo_all = lax.broadcasted_iota(jnp.int32, (size, 128), 1) < 64
+            for pair in range(heads // 2):
+                at = slice(pair * 128, pair * 128 + 128)
+                q = unit_rows(acc[0, 0:size, at])
+                k = unit_rows(acc[1, 0:size, at])
+                v = unit_rows(acc[2, 0:size, at])
+                d = jnp.where(live, k - v, 0.0)
+                k = jnp.where(live, k, 0.0)
+                rolled = pltpu.roll(d, 64, 1)
+                even = jnp.where(lo_all, q, pltpu.roll(k, 64, 1)).astype(bf)
+                odd = jnp.where(lo_all, pltpu.roll(q, 64, 1), k).astype(bf)
                 half_lo = lo[0 : MB // 2]
-                stg[2 * pair, ct, 0:64] = even[ct * MB : ct * MB + MB]
-                stg[2 * pair, ct, 64:96] = jnp.where(half_lo, d[top], rolled[bot]).astype(bf)
-                stg[2 * pair + 1, ct, 0:64] = odd[ct * MB : ct * MB + MB]
-                stg[2 * pair + 1, ct, 64:96] = jnp.where(half_lo, rolled[top], d[bot]).astype(bf)
-
-            give(2 * pair)
-            give(2 * pair + 1)
+                for n in range(part_size[p]):
+                    ct = part_first[p] + n
+                    top = slice(n * MB, n * MB + MB // 2)
+                    bot = slice(n * MB + MB // 2, n * MB + MB)
+                    stg[2 * pair, ct, 0:64] = even[n * MB : n * MB + MB]
+                    stg[2 * pair, ct, 64:96] = jnp.where(half_lo, d[top], rolled[bot]).astype(bf)
+                    stg[2 * pair + 1, ct, 0:64] = odd[n * MB : n * MB + MB]
+                    stg[2 * pair + 1, ct, 64:96] = jnp.where(half_lo, rolled[top], d[bot]).astype(bf)
+                give(2 * pair, p)
+                give(2 * pair + 1, p)
+
+        part(0)
+        part(1)
 
     def to_sibling(ct):
         return send(p1.at[ct], rs1.at[ct], rs1_s.at[ct], rs1_r.at[ct], dev(seg, sib, sec))
@@ -380,10 +401,16 @@
         return xl.at[pl.ds(number(g) * chunks, chunks)]
 
     def forward(g):
-        return send(three(g), three(g), fw_s.at[g], ch_r.at[number(g)], dev(seg, sib, sec))
+        return send(three(g), three(g), fw_s.at[g], fw_r.at[number(g)], dev(seg, sib, sec))
 
     def landed(g):
-        send(three(g), three(g), fw_s.at[0], ch_r.at[number(g)], dev(seg, sib, sec)).wait_recv()
+        send(three(g), three(g), fw_s.at[0], fw_r.at[number(g)], dev(seg, sib, sec)).wait_recv()
+
+    def came(g, p):
+        turned = lax.rem(c + sec, 2)
+        begin = (turned * (chunks - 1), 1 - turned)[p]
+        here = xl.at[pl.ds(number(g) * chunks + begin, part_size[p])]
+        send(here, here, fw_s.at[0], ch_r.at[number(g), p], dev(seg, sib, sec)).wait_recv()
 
     def exchange(g):
         return send(exs.at[g], exl.at[g], ex_s.at[g], ex_r.at[g], dev(seg, sib, sec))
@@ -408,8 +435,13 @@
         w[...] = w0
         wk[...] = w0.astype(bf)
         sc = ini[128:129]
-        landed(0)
-        forward(0).start()
+        came(0, 0)
+
+        @pl.when(sec == 1)
+        def _():
+            came(0, 1)
+            forward(0).start()
+
 
         z = dot(xl[at(0), 0:64], ub[0:128])
 
@@ -423,13 +455,25 @@
             give_back(i).start()
 
         def group(g, carry):
-            @pl.when(g < n_seg - 1)
+            ahead = jnp.where(sec == 1, 0, line // 2 - 1)
+
+            @pl.when(jnp.logical_and(g <= ahead, sec == 0))
+            def _():
+                came(g, 1)
+                forward(g).start()
+
+            @pl.when(g < line - 1)
+            def _():
+                came(g + 1, 0)
+
+            @pl.when(jnp.logical_and(g >= ahead, g < line - 1))
+            def _():
+                came(g + 1, 1)
+                forward(g + 1).start()
+
+            @pl.when(jnp.logical_and(g >= line - 1, g < n_seg - 1))
             def _():
                 landed(g + 1)
-
-            @pl.when(g < line - 1)
-            def _():
-                forward(g + 1).start()
 
             z, back = carry
             for t in range(chunks):
@@ -470,6 +514,7 @@
         aq = smooth(dot(last, ub[64:192])).astype(bf)
         mixed(n_seg, 0, pltpu.roll(last.astype(f32), 64, 1) + dot(aq, wk[...]))
 
+    def chain_drain():
         def drain(i, _):
             give_back(half + i).wait_send()
             return 0
@@ -503,11 +548,17 @@
         return 0
 
     lax.fori_loop(0, chunks, drain, 0)
+
+    @pl.when(in_chain)
+    def _():
+        chain_drain()
+
     for j in range(heads):
 
         @pl.when(jnp.logical_not(jnp.logical_and(holder, mine == j)))
         def _():
-            push(j).wait_send()
+            for p in range(2):
+                push(j, p).wait_send()
 
     @pl.when(holder)
     def _():
@@ -570,9 +621,10 @@
                 dma((n_head, chunks)),
                 dma((n_y, chunks)),
                 dma((chunks,)),
-                dma((heads,)),
+                dma((heads, 2)),
+                dma((n_seg, 2)),
+                dma((n_seg // 2,)),
                 dma((n_seg,)),
-                dma((n_seg // 2,)),
                 dma((n_seg // 2 + 1,)),
                 dma((n_seg // 2 + 1,)),
                 dma((nb // 2,)),

time: 143 us -> 136 us (0.951)
  Pallas kernels: 140 us -> 133 us
    pallas_call x1, Pallas kernels: 140 us -> 133 us  [local(): pl.pallas_call(functools.partial(kernel, n_seg, n_head, heads), out_shape...]
where the time goes in v5:
time: 136 us
  Pallas kernels  133 us (98%)
  local copies, waits for them, and re-layouts  1.59 us (1%)
    pallas_call x1, Pallas kernels, local(): pl.pallas_call(functools.partial(kernel, n_seg, n_head, heads), out_shape...  133 us

profile of v5, /device:TPU:4, one launch (start us, length us, event | category | flops | bytes accessed | tf_op | source)
XLA Modules:
  0.0 135.7 jit_solution(7167491383939561466)
XLA Ops:
  0.7 133.4 %both_groups.1 = bf16[1,192,384]{2,1,0:T(8,128)(2,1)} custom-call(bf16[192,384]{1,0:T(8,128)(2,1)} %tokens.1, bf16[1,3,3072,384]{3,2,1,0:T(8,128)(2,1)} %in_w.1, bf16[1,384,3072]{2,1,0:T(8,128)(2,1)} %out_w.1, f32[1,2,6,64,128]{4,3,2,1,0:T(8,128)} %expand.1, f32[1,2,6,64,128]{4,3,2,1,0:T(8,128)} %bitcast.1, f32[1,2,6]{2,1,0:T(2,128)} %rate.1, s32[1]{0:T(128)S(6)} %copy.9.counts), custom_call_target="tpu_custom_call" | custom-call | tf_op jit(solution)/shard_map/both_groups/pallas_call | solution.py:590
  134.1 1.6 %copy.10 = bf16[1,192,384]{2,1,0:T(8,128)(2,1)} copy(bf16[1,192,384]{2,1,0:T(8,128)(2,1)} %both_groups.1) | data formatting | bytes 294912

commit v6 on v5

--- a/solution.py
+++ b/solution.py
@@ -154,13 +154,8 @@
             loads.append(pltpu.make_async_copy(contract.at[0, way, mine], to.at[pl.ds(64, 64)], isem.at[len(loads)]))
         for copy in loads:
             copy.start()
-        every = rate[0]
-        at_way = lax.broadcasted_iota(jnp.int32, every.shape, 0)
-        at_head = lax.broadcasted_iota(jnp.int32, every.shape, 1)
         for way, to in ((c, ini), (1 - c, ini_s)):
-            picked = jnp.where((at_way == way) & (at_head == mine), every, 0.0)
-            one = jnp.sum(picked, axis=(0, 1), keepdims=True) * (1.0 / (64 * MB))
-            to[128:136] = jnp.broadcast_to(one, (8, 128))
+            to[128:136] = jnp.full((8, 128), rate[0, way, mine] * (1.0 / (64 * MB)), f32)
         for copy in loads:
             copy.wait()
 
@@ -290,14 +285,14 @@
                     acc[i, 0:size] = term if k == 0 else acc[i, 0:size] + term
 
             if p == 0:
-                lax.fori_loop(*times, spread, 0)
+                lax.fori_loop(0, chunks, spread, 0)
                 load_in.wait()
                 add(0)
-                lax.fori_loop(*times, relay, 0)
-                lax.fori_loop(1, chunks, spread, 0)
+                relay(0, 0)
             else:
+                relay(1, 0)
                 add(0)
-                lax.fori_loop(*times, relay, 0)
+                lax.fori_loop(2, chunks, relay, 0)
             for k in (1, 3, 2):
                 add(k)
             live = lax.broadcasted_iota(jnp.int32, (size, 128), 0) + begin < counts[0]
@@ -590,7 +585,7 @@
         return pl.pallas_call(
             functools.partial(kernel, n_seg, n_head, heads),
             out_shape=jax.ShapeDtypeStruct((1, rows, cols), bf),
-            in_specs=[any_space] * 5 + [vmem, smem],
+            in_specs=[any_space] * 5 + [smem, smem],
             out_specs=vmem,
             scratch_shapes=[
                 pltpu.VMEM(in_weight.shape[1:], bf),
@@ -637,7 +632,7 @@
                 dma,
             ],
             compiler_params=pltpu.CompilerParams(
-                collective_id=0, has_side_effects=True, vmem_limit_bytes=60 << 20
+                collective_id=0, has_side_effects=True, vmem_limit_bytes=55009 << 10
             ),
             name="both_groups",
         )(tokens, in_weight, out_weight, expand_init, jnp.swapaxes(contract_init, 3, 4), inner_rate, seg_counts)

time: 136 us -> 134 us (0.985)
  no operation moved by 1% of the time
where the time goes in v6:
time: 134 us
  Pallas kernels  132 us (99%)
  local copies, waits for them, and re-layouts  1.34 us (1%)
    pallas_call x1, Pallas kernels, local(): pl.pallas_call(functools.partial(kernel, n_seg, n_head, heads), out_shape...  132 us

profile of v6, /device:TPU:4, one launch (start us, length us, event | category | flops | bytes accessed | tf_op | source)
XLA Modules:
  0.0 134.2 jit_solution(14836519806292420526)
XLA Ops:
  0.7 0.0 copy-start
  0.7 0.7 copy-done
  1.3 132.2 %both_groups.1 = bf16[1,192,384]{2,1,0:T(8,128)(2,1)S(1)} custom-call(bf16[192,384]{1,0:T(8,128)(2,1)} %tokens.1, bf16[1,3,3072,384]{3,2,1,0:T(8,128)(2,1)} %in_w.1, bf16[1,384,3072]{2,1,0:T(8,128)(2,1)} %out_w.1, f32[1,2,6,64,128]{4,3,2,1,0:T(8,128)} %expand.1, f32[1,2,6,64,128]{4,3,2,1,0:T(8,128)} %bitcast.1, f32[1,2,6]{2,1,0:T(2,128)S(1)} %copy-done, ...), custom_call_target="tpu_custom_call" | custom-call | tf_op jit(solution)/shard_map/both_groups/pallas_call | solution.py:585
  133.5 0.7 copy.10
Async XLA Ops:
  0.7 0.7 copy-start

commit v7 on v6

--- a/solution.py
+++ b/solution.py
@@ -72,7 +72,7 @@
     inw, outw, hbuf, acc, stg, xl, ini_s, ini, exs, exl, mxs, mixb,
     p1, p2f, rs1, p2, rs2, u, w, ub, wk,
     wsem, tsem, isem, ag_s, ag_r, po_s, hop_s, push_s, ch_r, fw_s, fw_r, ex_s, ex_r,
-    mix_s, mix_r, rs1_s, rs1_r, rs2_s, rs2_r, ini_ss, ini_r,
+    mix_s, mix_r, rs1_s, rs1_r, rs2_s, rs2_r, ini_ss, ini_r, go,
 ):
     rows = tokens.shape[0]
     cols = tokens.shape[1]
@@ -89,10 +89,16 @@
     c = lax.rem(hd, 2)
     sib = 2 * y + 1 - c
     late = seg // line
+    from_end = seg + late * (n_seg - 1 - 2 * seg)
     spot = lax.rem(lax.rem(seg, line) + line - turn_by, line)
     in_chain = spot < heads
     cg = late
     mine = jnp.minimum(spot, heads - 1)
+
+    def mirror(f):
+        return f + late * (n_seg - 1 - 2 * f)
+
+    waves = ((1, (2, 3)), (3, (4, 5, 6, 7)))
 
     def place(group, j):
         return group * line + lax.rem(j + turn_by, line)
@@ -138,6 +144,13 @@
             @pl.when(jnp.logical_not(jnp.logical_and(holder, source == seg)))
             def _():
                 greet(dev(source, 2 * y + cg, sec))
+
+    for leader, followers in waves:
+        for follower in followers:
+
+            @pl.when(from_end == follower)
+            def _():
+                greet(dev(mirror(leader), hd, sec))
 
     @pl.when(sec == 1)
     def _():
@@ -165,6 +178,8 @@
 
     total = n_head - 1 + heads + (1 - sec)
     total = total + jnp.where(in_chain, line, 0) - jnp.where(holder, 1, 0)
+    for leader, followers in waves:
+        total = total + jnp.where(from_end == leader, len(followers), 0)
     pl.semaphore_wait(barrier, total)
 
     def direct(ct, k):
@@ -263,6 +278,16 @@
                 arrived(2 * lax.rem(y + k, n_y) + c, ct)
                 pass_on(ct, k).start()
             return 0
+
+        def lead(which):
+            leader, followers = waves[which]
+
+            @pl.when(from_end == leader)
+            def _():
+                for follower in followers:
+                    pl.semaphore_signal(
+                        go, inc=1, device_id=dev(mirror(follower), hd, sec), device_id_type=pl.DeviceIdType.MESH
+                    )
 
         def part(p):
             times = (0, 1) if p == 0 else (1, chunks)
@@ -295,6 +320,8 @@
                 lax.fori_loop(2, chunks, relay, 0)
             for k in (1, 3, 2):
                 add(k)
+            if p == 1:
+                lead(0)
             live = lax.broadcasted_iota(jnp.int32, (size, 128), 0) + begin < counts[0]
             lo_all = lax.broadcasted_iota(jnp.int32, (size, 128), 1) < 64
             for pair in range(heads // 2):
@@ -316,11 +343,26 @@
                     stg[2 * pair, ct, 64:96] = jnp.where(half_lo, d[top], rolled[bot]).astype(bf)
                     stg[2 * pair + 1, ct, 0:64] = odd[n * MB : n * MB + MB]
                     stg[2 * pair + 1, ct, 64:96] = jnp.where(half_lo, rolled[top], d[bot]).astype(bf)
-                give(2 * pair, p)
-                give(2 * pair + 1, p)
+                if p == 0:
+                    give(2 * pair, p)
+                    give(2 * pair + 1, p)
+                else:
+
+                    @pl.when(from_end < 2)
+                    def _():
+                        give(2 * pair, p)
+                        give(2 * pair + 1, p)
+
 
         part(0)
         part(1)
+
+        @pl.when(from_end >= 2)
+        def _():
+            pl.semaphore_wait(go, 1)
+            lead(1)
+            for j in range(heads):
+                give(j, 1)
 
     def to_sibling(ct):
         return send(p1.at[ct], rs1.at[ct], rs1_s.at[ct], rs1_r.at[ct], dev(seg, sib, sec))
@@ -630,6 +672,7 @@
                 dma((n_y, chunks)),
                 dma,
                 dma,
+                pltpu.SemaphoreType.REGULAR,
             ],
             compiler_params=pltpu.CompilerParams(
                 collective_id=0, has_side_effects=True, vmem_limit_bytes=55009 << 10

time: 134 us -> 134 us (level)
  no operation moved by 1% of the time
where the time goes in v7:
time: 134 us
  Pallas kernels  132 us (99%)
  local copies, waits for them, and re-layouts  1.34 us (1%)
    pallas_call x1, Pallas kernels, local(): pl.pallas_call(functools.partial(kernel, n_seg, n_head, heads), out_shape...  132 us

profile of v7, /device:TPU:4, one launch (start us, length us, event | category | flops | bytes accessed | tf_op | source)
XLA Modules:
  0.0 133.5 jit_solution(4061524727380643416)
XLA Ops:
  0.7 0.0 copy-start
  0.7 0.7 copy-done
  1.3 131.5 %both_groups.1 = bf16[1,192,384]{2,1,0:T(8,128)(2,1)S(1)} custom-call(bf16[192,384]{1,0:T(8,128)(2,1)} %tokens.1, bf16[1,3,3072,384]{3,2,1,0:T(8,128)(2,1)} %in_w.1, bf16[1,384,3072]{2,1,0:T(8,128)(2,1)} %out_w.1, f32[1,2,6,64,128]{4,3,2,1,0:T(8,128)} %expand.1, f32[1,2,6,64,128]{4,3,2,1,0:T(8,128)} %bitcast.1, f32[1,2,6]{2,1,0:T(2,128)S(1)} %copy-done, ...), custom_call_target="tpu_custom_call" | custom-call | tf_op jit(solution)/shard_map/both_groups/pallas_call | solution.py:627
  132.9 0.7 copy.10
Async XLA Ops:
  0.7 0.7 copy-start

commit v8 on v7

--- a/solution.py
+++ b/solution.py
@@ -396,7 +396,7 @@
 
         def reduce(ct):
             to_sibling(ct).wait_recv()
-            for k in (1, 3, 2):
+            for k in (2, 1, 3):
                 p2[ct, k] = (p2f[ct, k] + rs1[ct, k].astype(f32)).astype(bf)
                 to_chip(ct, k).start()
 
@@ -544,12 +544,12 @@
 
         carry = lax.fori_loop(0, n_seg, group, (z, jnp.zeros((64, 128), bf)))
         exchange(0).wait_recv()
-        for t in range(chunks):
-            mixed(n_seg - 1, t, exs[n_seg - 1, t])
         last = xl[at(nb - 1), 0:64]
         ub[64:128] = (u[...] - dot_tn(last, carry[1])[64:128]).astype(bf)
         aq = smooth(dot(last, ub[64:192])).astype(bf)
         mixed(n_seg, 0, pltpu.roll(last.astype(f32), 64, 1) + dot(aq, wk[...]))
+        for t in range(chunks):
+            mixed(n_seg - 1, chunks - 1 - t, exs[n_seg - 1, chunks - 1 - t])
 
     def chain_drain():
         def drain(i, _):

time: 134 us -> 134 us (level)
  no operation moved by 1% of the time
where the time goes in v8:
time: 134 us; the launch traced here: 133 us
  Pallas kernels  131 us (98%)
  local copies, waits for them, and re-layouts  1.34 us (1%)
    pallas_call x1, Pallas kernels, local(): pl.pallas_call(functools.partial(kernel, n_seg, n_head, heads), out_shape...  131 us

profile of v8, /device:TPU:4, one launch (start us, length us, event | category | flops | bytes accessed | tf_op | source)
XLA Modules:
  0.0 133.4 jit_solution(9509119741620046376)
XLA Ops:
  0.7 0.0 copy-start
  0.7 0.7 copy-done
  1.3 131.4 %both_groups.1 = bf16[1,192,384]{2,1,0:T(8,128)(2,1)S(1)} custom-call(bf16[192,384]{1,0:T(8,128)(2,1)} %tokens.1, bf16[1,3,3072,384]{3,2,1,0:T(8,128)(2,1)} %in_w.1, bf16[1,384,3072]{2,1,0:T(8,128)(2,1)} %out_w.1, f32[1,2,6,64,128]{4,3,2,1,0:T(8,128)} %expand.1, f32[1,2,6,64,128]{4,3,2,1,0:T(8,128)} %bitcast.1, f32[1,2,6]{2,1,0:T(2,128)S(1)} %copy-done, ...), custom_call_target="tpu_custom_call" | custom-call | tf_op jit(solution)/shard_map/both_groups/pallas_call | solution.py:627
  132.7 0.7 copy.10
Async XLA Ops:
  0.7 0.7 copy-start
